TPU v7x, 512 devices: a whole 4x8x8 slice. The times are simulated.
512 devices in a mesh: gx: 32 (over x, y), gy: 16 (over z, core).
Axes of the slice: x: 4, y: 8, z: 8, core: 2. Of those that a mesh axis runs over, the one named last changes fastest.
Arguments:
- snapshots: float32 [262144, 512], P(('gx', 'gy')), may hold values from -900 to 900
Outputs:
- dmd_operator: float32 [511, 511], replicated
- coefficients: float32 [511], replicated
- basis: float32 [262144, 512], P(('gx', 'gy'))
All inputs are finite; a program needn't handle non-finite values.
Results may differ from a plain program's by a relative error of at most 0.0003.
Values sent between devices are 32-bit elements; how exact they have to be, the bound alone decides.
No kernel may reach another device: no remote copies, remote signals or barrier semaphores. Data moves between devices by JAX's collectives and lax.ppermute only.
A program may use at most 64 MiB of HBM per device.

v0:
```python
import math

import jax
import jax.numpy as jnp
from jax import lax
from jax.sharding import PartitionSpec as P


def partner_2(block, axis, stride):
    count = lax.axis_size(axis)
    route = []
    for low in range(count):
        high = low | 1 << stride
        if high != low and high < count:
            route += [(low, high), (high, low)]
    return lax.ppermute(block, axis, route)


def exact_dot(left_side, right_side):
    return jnp.dot(
        left_side, right_side, precision=lax.Precision.HIGHEST, preferred_element_type=jnp.float32
    )


def square_products(left_side):
    return lax.dot_general(
        left_side,
        left_side,
        (((0,), (0,)), ((), ())),
        precision=lax.Precision.HIGHEST,
        preferred_element_type=jnp.float32,
    )


def small_cholesky(block):
    width_n = block.shape[0]
    positions = lax.iota(jnp.int32, width_n)

    def column_step(j, carry):
        work, lower = carry
        column = lax.dynamic_slice_in_dim(work, j, 1, 1)[:, 0]
        pivot = jnp.sqrt(lax.dynamic_slice_in_dim(column, j, 1, 0)[0])
        vector = jnp.where(positions >= j, column / pivot, 0.0)
        lower = lax.dynamic_update_slice_in_dim(lower, vector[:, None], j, 1)
        work = work - vector[:, None] * vector[None, :]
        return (work, lower)

    _, lower = lax.fori_loop(0, width_n, column_step, (block, jnp.zeros_like(block)))
    return lower


def small_lower_inverse(lower):
    width_n = lower.shape[0]
    positions = lax.iota(jnp.int32, width_n)

    def row_step(i, inverse):
        row_vals = lax.dynamic_slice_in_dim(lower, i, 1, 0)
        pivot = lax.dynamic_slice_in_dim(row_vals[0], i, 1, 0)[0]
        unit_row = (positions == i).astype(jnp.float32)[None, :]
        new_row = (unit_row - exact_dot(row_vals, inverse)) / pivot
        return lax.dynamic_update_slice_in_dim(inverse, new_row, i, 0)

    return lax.fori_loop(0, width_n, row_step, jnp.zeros_like(lower))


def factor_with_inverse(products):
    width_m = products.shape[0]
    block_size = 64
    work = products
    lower = jnp.zeros_like(products)
    block_inverses = []
    for block_id in range(width_m // block_size):
        start = block_id * block_size
        stop = start + block_size
        diag_low = small_cholesky(work[start:stop, start:stop])
        diag_inv = small_lower_inverse(diag_low)
        lower = lower.at[start:stop, start:stop].set(diag_low)
        if stop < width_m:
            panel = exact_dot(work[stop:, start:stop], diag_inv.T)
            lower = lower.at[stop:, start:stop].set(panel)
            work = work.at[stop:, stop:].add(-exact_dot(panel, panel.T))
        block_inverses.append(diag_inv)
    inverse = jnp.zeros_like(products)
    for block_id in range(width_m // block_size):
        start = block_id * block_size
        stop = start + block_size
        inverse = inverse.at[start:stop, start:stop].set(block_inverses[block_id])
        if start > 0:
            inner_part = exact_dot(lower[start:stop, :start], inverse[:start, :start])
            inverse = inverse.at[start:stop, :start].set(
                -exact_dot(block_inverses[block_id], inner_part)
            )
    return (lower.T, inverse.T)


def swap_inner(matrix, bit_index):
    return partner_2(matrix, "gy", bit_index)


def swap_outer(matrix, bit_index):
    return partner_2(matrix, "gx", bit_index)


def combine_pair(state, partner, pooled, needed_rows):
    factor_now, inverse_now = state
    factor_now = factor_now + partner
    if 2 * pooled >= needed_rows:
        factor_now, inverse_now = factor_with_inverse(factor_now)
    return ((factor_now, inverse_now), 2 * pooled)


def inner_sections(state, pooled, needed_rows):
    for bit_index in range(lax.axis_size("gy").bit_length() - 1):
        partner = swap_inner(state[0], bit_index)
        state, pooled = combine_pair(state, partner, pooled, needed_rows)
    return (state, pooled)


def outer_sections(state, pooled, needed_rows):
    for bit_index in range(lax.axis_size("gx").bit_length() - 1):
        partner = swap_outer(state[0], bit_index)
        state, pooled = combine_pair(state, partner, pooled, needed_rows)
    return (state, pooled)


def body(snapshots):
    width_m = snapshots.shape[1]
    local_gram = square_products(snapshots)
    needed_rows = 512 * width_m
    pooled = snapshots.shape[0]
    state = (local_gram, local_gram)
    state, pooled = inner_sections(state, pooled, needed_rows)
    state, pooled = outer_sections(state, pooled, needed_rows)
    factor, inverse = state
    kept_cols = width_m - 1
    lead_inverse = inverse[:kept_cols, :kept_cols]
    dmd_operator = exact_dot(factor[:kept_cols, 1:], lead_inverse)
    coefficients = exact_dot(lead_inverse, factor[:kept_cols, kept_cols])
    row_total = snapshots.shape[0] * lax.axis_size("gx") * lax.axis_size("gy")
    basis = exact_dot(snapshots, inverse) * math.sqrt(row_total)
    return (dmd_operator, coefficients, basis)


def solution(mesh):
    placed = (P(("gx", "gy"), None),)
    return jax.shard_map(
        body,
        mesh=mesh,
        in_specs=placed,
        out_specs=(P(), P(), P(("gx", "gy"), None)),
        check_vma=False,
    )
```

profile of v0, /device:TPU:1, one launch (start us, length us, event | category | flops | bytes accessed | tf_op | source)
XLA Modules:
  0.0 1828.9 jit_solution(16145898062249206359)
XLA Ops:
  0.6 1.2 copy-done
  1.9 1.9 fusion.129
  3.7 8.8 collective-permute-start
  12.5 2.3 collective-permute-done
  15.0 1.9 collective-permute-start.1
  16.9 24.3 %collective-permute-done.1 = f32[512,512]{0,1:T(8,128)S(1)} collective-permute-done((f32[512,512]{0,1:T(8,128)S(1)}, f32[512,512]{0,1:T(8,128)S(1)}, u32[]{:S(2)}, u32[]{:S(2)}) %collective-permute-start.1) | collective-permute-done | bytes 1048608 | tf_op jit(solution)/shard_map/ppermute | solution.py:16
  41.5 1.9 collective-permute-start.2
  43.4 48.4 %collective-permute-done.2 = f32[512,512]{0,1:T(8,128)S(1)} collective-permute-done((f32[512,512]{0,1:T(8,128)S(1)}, f32[512,512]{0,1:T(8,128)S(1)}, u32[]{:S(2)}, u32[]{:S(2)}) %collective-permute-start.2) | collective-permute-done | bytes 1048608 | tf_op jit(solution)/shard_map/ppermute | solution.py:16
  92.0 4.3 collective-permute-start.3
  96.3 48.3 %collective-permute-done.3 = f32[512,512]{0,1:T(8,128)S(1)} collective-permute-done((f32[512,512]{0,1:T(8,128)S(1)}, f32[512,512]{0,1:T(8,128)S(1)}, u32[]{:S(2)}, u32[]{:S(2)}) %collective-permute-start.3) | collective-permute-done | bytes 1048608 | tf_op jit(solution)/shard_map/ppermute | solution.py:16
  144.9 1.9 collective-permute-start.4
  146.8 24.2 %collective-permute-done.4 = f32[512,512]{0,1:T(8,128)S(1)} collective-permute-done((f32[512,512]{0,1:T(8,128)S(1)}, f32[512,512]{0,1:T(8,128)S(1)}, u32[]{:S(2)}, u32[]{:S(2)}) %collective-permute-start.4) | collective-permute-done | bytes 1048608 | tf_op jit(solution)/shard_map/ppermute | solution.py:16
  171.2 1.9 collective-permute-start.5
  173.2 48.4 %collective-permute-done.5 = f32[512,512]{0,1:T(8,128)S(1)} collective-permute-done((f32[512,512]{0,1:T(8,128)S(1)}, f32[512,512]{0,1:T(8,128)S(1)}, u32[]{:S(2)}, u32[]{:S(2)}) %collective-permute-start.5) | collective-permute-done | bytes 1048608 | tf_op jit(solution)/shard_map/ppermute | solution.py:16
  221.7 2.2 collective-permute-start.6
  223.9 47.9 %collective-permute-done.6 = f32[512,512]{0,1:T(8,128)S(1)} collective-permute-done((f32[512,512]{0,1:T(8,128)S(1)}, f32[512,512]{0,1:T(8,128)S(1)}, u32[]{:S(2)}, u32[]{:S(2)}) %collective-permute-start.6) | collective-permute-done | bytes 1048608 | tf_op jit(solution)/shard_map/ppermute | solution.py:16
  272.0 1.9 collective-permute-start.7
  273.9 23.2 %collective-permute-done.7 = f32[512,512]{0,1:T(8,128)S(1)} collective-permute-done((f32[512,512]{0,1:T(8,128)S(1)}, f32[512,512]{0,1:T(8,128)S(1)}, u32[]{:S(2)}, u32[]{:S(2)}) %collective-permute-start.7) | collective-permute-done | bytes 1048608 | tf_op jit(solution)/shard_map/ppermute | solution.py:16
  297.4 2.6 collective-permute-start.8
  299.9 23.3 %collective-permute-done.8 = f32[512,512]{0,1:T(8,128)} collective-permute-done((f32[512,512]{0,1:T(8,128)S(1)}, f32[512,512]{0,1:T(8,128)}, u32[]{:S(2)}, u32[]{:S(2)}) %collective-permute-start.8) | collective-permute-done | bytes 1048608 | tf_op jit(solution)/shard_map/ppermute | solution.py:16
  323.2 1.4 add.852
  324.7 86.0 %while.325 = (s32[]{:T(128)}, f32[64,64]{0,1:T(8,128)S(1)}, f32[64,64]{0,1:T(8,128)S(1)}, s32[]{:T(128)}, s32[]{:T(128)}, /*index=5*/s32[]{:T(128)}) while((s32[]{:T(128)}, f32[64,64]{0,1:T(8,128)S(1)}, f32[64,64]{0,1:T(8,128)S(1)}, s32[]{:T(128)}, s32[]{:T(128)}, /*index=5*/s32[]{:T(128)}) %tuple.810), condition=%wide.region_1.2_spmd.clone, body=%wide.region_0.1_spmd.clone.sunk | while | flops 8515 | bytes 36221 | solution.py:48
  410.9 90.5 %while.326 = (s32[]{:T(128)}, f32[64,64]{1,0:T(8,128)S(1)}, f32[64,64]{1,0:T(8,128)S(1)}, s32[]{:T(128)}, s32[]{:T(128)}, /*index=5*/s32[]{:T(128)}) while((s32[]{:T(128)}, f32[64,64]{1,0:T(8,128)S(1)}, f32[64,64]{1,0:T(8,128)S(1)}, s32[]{:T(128)}, s32[]{:T(128)}, /*index=5*/s32[]{:T(128)}) %tuple.813), condition=%wide.region_3.4_spmd.clone, body=%wide.region_2.3_spmd.clone.sunk | while | flops 49411 | bytes 35185 | solution.py:63
  503.7 91.5 %while.327 = (s32[]{:T(128)}, f32[64,64]{0,1:T(8,128)S(1)}, f32[64,64]{0,1:T(8,128)S(1)}, s32[]{:T(128)}, s32[]{:T(128)}, /*index=5*/s32[]{:T(128)}) while((s32[]{:T(128)}, f32[64,64]{0,1:T(8,128)S(1)}, f32[64,64]{0,1:T(8,128)S(1)}, s32[]{:T(128)}, s32[]{:T(128)}, /*index=5*/s32[]{:T(128)}) %tuple.816), condition=%wide.region_5.6_spmd.clone, body=%wide.region_4.5_spmd.clone.sunk | while | flops 8515 | bytes 36221 | solution.py:48
  595.3 2.1 scatter.101
  597.3 1.4 scatter.104
  598.8 90.5 %while.328 = (s32[]{:T(128)}, f32[64,64]{1,0:T(8,128)S(1)}, f32[64,64]{1,0:T(8,128)S(1)}, s32[]{:T(128)}, s32[]{:T(128)}, /*index=5*/s32[]{:T(128)}) while((s32[]{:T(128)}, f32[64,64]{1,0:T(8,128)S(1)}, f32[64,64]{1,0:T(8,128)S(1)}, s32[]{:T(128)}, s32[]{:T(128)}, /*index=5*/s32[]{:T(128)}) %tuple.819), condition=%wide.region_7.8_spmd.clone, body=%wide.region_6.7_spmd.clone.sunk | while | flops 49411 | bytes 35185 | solution.py:63
  689.3 1.2 constant_dynamic-update-slice_fusion.2
  692.1 91.4 %while.329 = (s32[]{:T(128)}, f32[64,64]{0,1:T(8,128)S(1)}, f32[64,64]{0,1:T(8,128)S(1)}, s32[]{:T(128)}, s32[]{:T(128)}, /*index=5*/s32[]{:T(128)}) while((s32[]{:T(128)}, f32[64,64]{0,1:T(8,128)S(1)}, f32[64,64]{0,1:T(8,128)S(1)}, s32[]{:T(128)}, s32[]{:T(128)}, /*index=5*/s32[]{:T(128)}) %tuple.822), condition=%wide.region_9.10_spmd.clone, body=%wide.region_8.9_spmd.clone.sunk | while | flops 8515 | bytes 36221 | solution.py:48
  783.6 90.5 %while.330 = (s32[]{:T(128)}, f32[64,64]{1,0:T(8,128)S(1)}, f32[64,64]{1,0:T(8,128)S(1)}, s32[]{:T(128)}, s32[]{:T(128)}, /*index=5*/s32[]{:T(128)}) while((s32[]{:T(128)}, f32[64,64]{1,0:T(8,128)S(1)}, f32[64,64]{1,0:T(8,128)S(1)}, s32[]{:T(128)}, s32[]{:T(128)}, /*index=5*/s32[]{:T(128)}) %tuple.825), condition=%wide.region_11.12_spmd.clone, body=%wide.region_10.11_spmd.clone.sunk | while | flops 49411 | bytes 35185 | solution.py:63
  874.2 1.2 fusion.111
  875.4 1.6 fusion.81
  877.0 91.5 %while.331 = (s32[]{:T(128)}, f32[64,64]{0,1:T(8,128)S(1)}, f32[64,64]{0,1:T(8,128)S(1)}, s32[]{:T(128)}, s32[]{:T(128)}, /*index=5*/s32[]{:T(128)}) while((s32[]{:T(128)}, f32[64,64]{0,1:T(8,128)S(1)}, f32[64,64]{0,1:T(8,128)S(1)}, s32[]{:T(128)}, s32[]{:T(128)}, /*index=5*/s32[]{:T(128)}) %tuple.828), condition=%wide.region_13.14_spmd.clone, body=%wide.region_12.13_spmd.clone.sunk | while | flops 8515 | bytes 36221 | solution.py:48
  968.6 1.1 scatter.106
  969.7 1.8 scatter.109
  971.4 1.4 scatter.110
  972.9 90.5 %while.332 = (s32[]{:T(128)}, f32[64,64]{1,0:T(8,128)S(1)}, f32[64,64]{1,0:T(8,128)S(1)}, s32[]{:T(128)}, s32[]{:T(128)}, /*index=5*/s32[]{:T(128)}) while((s32[]{:T(128)}, f32[64,64]{1,0:T(8,128)S(1)}, f32[64,64]{1,0:T(8,128)S(1)}, s32[]{:T(128)}, s32[]{:T(128)}, /*index=5*/s32[]{:T(128)}) %tuple.831), condition=%wide.region_15.16_spmd.clone, body=%wide.region_14.15_spmd.clone.sunk | while | flops 49411 | bytes 35185 | solution.py:63
  1064.2 91.5 %while.333 = (s32[]{:T(128)}, f32[64,64]{0,1:T(8,128)S(1)}, f32[64,64]{0,1:T(8,128)S(1)}, s32[]{:T(128)}, s32[]{:T(128)}, /*index=5*/s32[]{:T(128)}) while((s32[]{:T(128)}, f32[64,64]{0,1:T(8,128)S(1)}, f32[64,64]{0,1:T(8,128)S(1)}, s32[]{:T(128)}, s32[]{:T(128)}, /*index=5*/s32[]{:T(128)}) %tuple.834), condition=%wide.region_17.18_spmd.clone, body=%wide.region_16.17_spmd.clone.sunk | while | flops 8515 | bytes 36221 | solution.py:48
  1155.7 90.5 %while.334 = (s32[]{:T(128)}, f32[64,64]{1,0:T(8,128)S(1)}, f32[64,64]{1,0:T(8,128)S(1)}, s32[]{:T(128)}, s32[]{:T(128)}, /*index=5*/s32[]{:T(128)}) while((s32[]{:T(128)}, f32[64,64]{1,0:T(8,128)S(1)}, f32[64,64]{1,0:T(8,128)S(1)}, s32[]{:T(128)}, s32[]{:T(128)}, /*index=5*/s32[]{:T(128)}) %tuple.837), condition=%wide.region_19.20_spmd.clone, body=%wide.region_18.19_spmd.clone.sunk | while | flops 49411 | bytes 35185 | solution.py:63
  1247.0 91.5 %while.335 = (s32[]{:T(128)}, f32[64,64]{0,1:T(8,128)S(1)}, f32[64,64]{0,1:T(8,128)S(1)}, s32[]{:T(128)}, s32[]{:T(128)}, /*index=5*/s32[]{:T(128)}) while((s32[]{:T(128)}, f32[64,64]{0,1:T(8,128)S(1)}, f32[64,64]{0,1:T(8,128)S(1)}, s32[]{:T(128)}, s32[]{:T(128)}, /*index=5*/s32[]{:T(128)}) %tuple.840), condition=%wide.region_21.22_spmd.clone, body=%wide.region_20.21_spmd.clone.sunk | while | flops 8515 | bytes 36221 | solution.py:48
  1338.5 1.1 scatter.114
  1339.6 1.4 scatter.115
  1341.0 1.4 scatter.116
  1342.5 90.5 %while.336 = (s32[]{:T(128)}, f32[64,64]{1,0:T(8,128)S(1)}, f32[64,64]{1,0:T(8,128)S(1)}, s32[]{:T(128)}, s32[]{:T(128)}, /*index=5*/s32[]{:T(128)}) while((s32[]{:T(128)}, f32[64,64]{1,0:T(8,128)S(1)}, f32[64,64]{1,0:T(8,128)S(1)}, s32[]{:T(128)}, s32[]{:T(128)}, /*index=5*/s32[]{:T(128)}) %tuple.843), condition=%wide.region_23.24_spmd.clone, body=%wide.region_22.23_spmd.clone.sunk | while | flops 49411 | bytes 35185 | solution.py:63
  1433.6 91.5 %while.337 = (s32[]{:T(128)}, f32[64,64]{0,1:T(8,128)S(1)}, f32[64,64]{0,1:T(8,128)S(1)}, s32[]{:T(128)}, s32[]{:T(128)}, /*index=5*/s32[]{:T(128)}) while((s32[]{:T(128)}, f32[64,64]{0,1:T(8,128)S(1)}, f32[64,64]{0,1:T(8,128)S(1)}, s32[]{:T(128)}, s32[]{:T(128)}, /*index=5*/s32[]{:T(128)}) %tuple.846), condition=%wide.region_25.26_spmd.clone, body=%wide.region_24.25_spmd.clone.sunk | while | flops 8515 | bytes 36221 | solution.py:48
  1525.2 90.5 %while.338 = (s32[]{:T(128)}, f32[64,64]{1,0:T(8,128)S(1)}, f32[64,64]{1,0:T(8,128)S(1)}, s32[]{:T(128)}, s32[]{:T(128)}, /*index=5*/s32[]{:T(128)}) while((s32[]{:T(128)}, f32[64,64]{1,0:T(8,128)S(1)}, f32[64,64]{1,0:T(8,128)S(1)}, s32[]{:T(128)}, s32[]{:T(128)}, /*index=5*/s32[]{:T(128)}) %tuple.849), condition=%wide.region_27.28_spmd.clone, body=%wide.region_26.27_spmd.clone.sunk | while | flops 49411 | bytes 35185 | solution.py:63
  1616.3 91.5 %while.339 = (s32[]{:T(128)}, f32[64,64]{0,1:T(8,128)S(1)}, f32[64,64]{0,1:T(8,128)S(1)}, s32[]{:T(128)}, s32[]{:T(128)}, /*index=5*/s32[]{:T(128)}) while((s32[]{:T(128)}, f32[64,64]{0,1:T(8,128)S(1)}, f32[64,64]{0,1:T(8,128)S(1)}, s32[]{:T(128)}, s32[]{:T(128)}, /*index=5*/s32[]{:T(128)}) %tuple.852), condition=%wide.region_29.30_spmd.clone, body=%wide.region_28.29_spmd.clone.sunk | while | flops 8515 | bytes 36221 | solution.py:48
  1708.6 1.1 scatter.121
  1709.8 1.0 scatter.124
  1710.9 1.4 scatter.126
  1712.8 1.1 scatter.129
  1713.9 1.1 scatter.130
  1715.5 1.7 scatter.134
  1717.8 1.6 scatter.135
  1719.4 1.1 scatter.136
  1721.1 1.4 scatter.140
  1723.3 1.7 scatter.141
  1726.7 90.5 %while.340 = (s32[]{:T(128)}, f32[64,64]{1,0:T(8,128)S(1)}, f32[64,64]{1,0:T(8,128)S(1)}, s32[]{:T(128)}, s32[]{:T(128)}, /*index=5*/s32[]{:T(128)}) while((s32[]{:T(128)}, f32[64,64]{1,0:T(8,128)S(1)}, f32[64,64]{1,0:T(8,128)S(1)}, s32[]{:T(128)}, s32[]{:T(128)}, /*index=5*/s32[]{:T(128)}) %tuple.855), condition=%wide.region_31.32_spmd.clone, body=%wide.region_30.31_spmd.clone.sunk | while | flops 49411 | bytes 35185 | solution.py:63
  1817.2 1.0 scatter.146
  1819.2 1.2 scatter.149
  1820.6 2.8 fusion.80
  1823.5 2.9 fusion.89
  1826.3 1.3 fusion.91
  1827.6 1.3 copy.43
  (4175 shorter events, 1091.0 us)
Async XLA Ops:
  0.6 1.2 copy-start
  3.7 11.1 collective-permute-start
  15.0 26.3 %collective-permute-start.1 = (f32[512,512]{0,1:T(8,128)S(1)}, f32[512,512]{0,1:T(8,128)S(1)}, u32[]{:S(2)}, u32[]{:S(2)}) collective-permute-start(f32[512,512]{0,1:T(8,128)S(1)} %add.844), channel_id=1, source_target_pairs={{0,2},{2,0},{1,3},{3,1},{4,6},{6,4},{5,7},{7,5},{8,10},{10,8},{9,1... | collective-permute-start | bytes 3145736 | tf_op jit(solution)/shard_map/ppermute | solution.py:16
  41.5 50.3 %collective-permute-start.2 = (f32[512,512]{0,1:T(8,128)S(1)}, f32[512,512]{0,1:T(8,128)S(1)}, u32[]{:S(2)}, u32[]{:S(2)}) collective-permute-start(f32[512,512]{0,1:T(8,128)S(1)} %add.845), channel_id=1, source_target_pairs={{0,4},{4,0},{1,5},{5,1},{2,6},{6,2},{3,7},{7,3},{8,12},{12,8},{9,1... | collective-permute-start | bytes 3145736 | tf_op jit(solution)/shard_map/ppermute | solution.py:16
  92.0 52.7 %collective-permute-start.3 = (f32[512,512]{0,1:T(8,128)S(1)}, f32[512,512]{0,1:T(8,128)S(1)}, u32[]{:S(2)}, u32[]{:S(2)}) collective-permute-start(f32[512,512]{0,1:T(8,128)S(1)} %add.846), channel_id=1, source_target_pairs={{0,8},{8,0},{1,9},{9,1},{2,10},{10,2},{3,11},{11,3},{4,12},{12,4},... | collective-permute-start | bytes 3145736 | tf_op jit(solution)/shard_map/ppermute | solution.py:16
  144.9 26.1 %collective-permute-start.4 = (f32[512,512]{0,1:T(8,128)S(1)}, f32[512,512]{0,1:T(8,128)S(1)}, u32[]{:S(2)}, u32[]{:S(2)}) collective-permute-start(f32[512,512]{0,1:T(8,128)S(1)} %add.847), channel_id=1, source_target_pairs={{0,16},{16,0},{32,48},{48,32},{64,80},{80,64},{96,112},{112,96},{1... | collective-permute-start | bytes 3145736 | tf_op jit(solution)/shard_map/ppermute | solution.py:16
  171.2 50.3 %collective-permute-start.5 = (f32[512,512]{0,1:T(8,128)S(1)}, f32[512,512]{0,1:T(8,128)S(1)}, u32[]{:S(2)}, u32[]{:S(2)}) collective-permute-start(f32[512,512]{0,1:T(8,128)S(1)} %add.848), channel_id=1, source_target_pairs={{0,32},{32,0},{16,48},{48,16},{64,96},{96,64},{80,112},{112,80},{1... | collective-permute-start | bytes 3145736 | tf_op jit(solution)/shard_map/ppermute | solution.py:16
  221.7 50.0 %collective-permute-start.6 = (f32[512,512]{0,1:T(8,128)S(1)}, f32[512,512]{0,1:T(8,128)S(1)}, u32[]{:S(2)}, u32[]{:S(2)}) collective-permute-start(f32[512,512]{0,1:T(8,128)S(1)} %add.849), channel_id=1, source_target_pairs={{0,64},{64,0},{16,80},{80,16},{32,96},{96,32},{48,112},{112,48},{1... | collective-permute-start | bytes 3145736 | tf_op jit(solution)/shard_map/ppermute | solution.py:16
  272.0 25.2 %collective-permute-start.7 = (f32[512,512]{0,1:T(8,128)S(1)}, f32[512,512]{0,1:T(8,128)S(1)}, u32[]{:S(2)}, u32[]{:S(2)}) collective-permute-start(f32[512,512]{0,1:T(8,128)S(1)} %add.850), channel_id=1, source_target_pairs={{0,128},{128,0},{16,144},{144,16},{32,160},{160,32},{48,176},{176,... | collective-permute-start | bytes 3145736 | tf_op jit(solution)/shard_map/ppermute | solution.py:16
  297.4 25.9 %collective-permute-start.8 = (f32[512,512]{0,1:T(8,128)S(1)}, f32[512,512]{0,1:T(8,128)}, u32[]{:S(2)}, u32[]{:S(2)}) collective-permute-start(f32[512,512]{0,1:T(8,128)S(1)} %add.851), channel_id=1, source_target_pairs={{0,256},{256,0},{16,272},{272,16},{32,288},{288,32},{48,304},{304,... | collective-permute-start | bytes 3145736 | tf_op jit(solution)/shard_map/ppermute | solution.py:16
  502.8 0.9 copy-start.2
  503.7 186.8 %copy-start.3 = (f32[448,448]{0,1:T(8,128)S(1)}, f32[448,448]{0,1:T(8,128)}, u32[]{:S(2)}) copy-start(f32[448,448]{0,1:T(8,128)} %copy-done.2) | copy-start | bytes 2408452
  691.3 0.8 copy-start.4
  1826.3 1.3 copy-start.1
where the time goes:
time: 1840 us; the launch traced here: 1830 us
  local copies, waits for them, and re-layouts  663 us (36%)
  matrix products  422 us (23%)
  loops' own time  375 us (20%)
  waiting for transfers between devices  290 us (16%)
  other arithmetic  50.8 us (3%)
  starting transfers between devices  27.4 us (1%)
    dot_general x543, matrix products, exact_dot(): jnp.dot(left_side, right_side, precision=lax.Precision.HIGHEST, preferred...  420 us
    another operation x8, loops' own time, small_cholesky(): lax.fori_loop(0, width_n, column_step, (block, jnp.zeros_like(block)))  365 us
    dynamic_slice x512, local copies, waits for them, and re-layouts, row_step(): pivot = lax.dynamic_slice_in_dim(row_vals[0], i, 1, 0)[0]  301 us
    dynamic_slice x512, local copies, waits for them, and re-layouts, column_step(): pivot = jnp.sqrt(lax.dynamic_slice_in_dim(column, j, 1, 0)[0])  301 us
    ppermute x9, waiting for transfers between devices, partner_2(): return lax.ppermute(block, axis, route)  290 us
    sub x512, other arithmetic, column_step(): work = work - vector[:, None] * vector[None, :]  38.5 us

commit v1 on v0

v1 whole, which is shorter than its diff:
```python
import functools
import math

import jax
import jax.numpy as jnp
from jax import lax
from jax.experimental import pallas as pl
from jax.experimental.pallas import tpu as pltpu
from jax.sharding import Mesh
from jax.sharding import PartitionSpec as P

F32 = jnp.float32
BF = jnp.bfloat16
NB = 128
SUB = 8


def dot6(x, y, dims):
    return lax.dot_general(
        x, y, (dims, ((), ())), precision=lax.Precision.HIGHEST, preferred_element_type=F32
    )


def block_rows(nblk):
    out = []
    for i in range(nblk):
        for j in range(i, nblk):
            out.append((i, j, len(out) * NB))
    return out


def gram_kernel(x_ref, out_ref):
    nblk = x_ref.shape[1] // NB
    at = {(i, j): row for i, j, row in block_rows(nblk)}
    for i in range(nblk):
        part = dot6(x_ref[:, i * NB : (i + 1) * NB], x_ref[:, i * NB :], ((0,), (0,)))
        for j in range(i, nblk):
            row = at[(i, j)]
            out_ref[row : row + NB, :] = part[:, (j - i) * NB : (j - i + 1) * NB]


def split3(x):
    a = x.astype(BF)
    rest = x - a.astype(F32)
    b = rest.astype(BF)
    c = (rest - b.astype(F32)).astype(BF)
    return a, b, c


def tn_small(x, y):
    xa, xb, xc = split3(x)
    ya, yb, yc = split3(y)
    left = jnp.concatenate([xa, xa, xb, xb, xa, xc], 0)
    right = jnp.concatenate([ya, yb, ya, yb, yc, ya], 0)
    return lax.dot_general(left, right, (((0,), (0,)), ((), ())), preferred_element_type=F32)


def row_of(x, k):
    return jnp.broadcast_to(x[k : k + 1, :], x.shape)


def lane_of(x, j):
    return jnp.broadcast_to(x[:, j : j + 1], x.shape)


def factor_block(tiles_in):
    tiles = NB // SUB
    sub = lax.broadcasted_iota(jnp.int32, (SUB, NB), 0)
    lane = lax.broadcasted_iota(jnp.int32, (SUB, NB), 1)
    a = list(tiles_in)
    us, ts = [], []
    for p in range(tiles):
        off = p * SUB
        inpanel = (lane >= off) & (lane < off + SUB)
        rows = [a[p]] + ([a[p + 1]] if p + 1 < tiles else [])
        cols = [[lane_of(r, off + j) for j in range(SUB)] for r in rows]
        aug = [jnp.where(inpanel, (lane == off + sub).astype(F32), rows[0])]
        if len(rows) > 1:
            aug.append(jnp.where(inpanel, 0.0, rows[1]))
        dvec = jnp.zeros((SUB, NB), F32)
        rvec = jnp.zeros((SUB, NB), F32)
        for k in range(SUB):
            d = row_of(cols[0][k], k)
            r = 1.0 / d
            dvec = jnp.where(sub == k, d, dvec)
            rvec = jnp.where(sub == k, r, rvec)
            mult = [jnp.where(sub > k, cols[0][k] * r, 0.0)]
            if len(rows) > 1:
                mult.append(cols[1][k] * r)
            for j in range(k + 1, SUB):
                b = row_of(cols[0][j], k)
                for q in range(len(rows)):
                    cols[q][j] = cols[q][j] - mult[q] * b
            b = row_of(aug[0], k)
            for q in range(len(rows)):
                aug[q] = aug[q] - mult[q] * b
        if len(rows) > 1:
            a[p + 1] = aug[1]
        if p + 2 < tiles:
            left = jnp.where(lane >= off + 2 * SUB, aug[0] * rvec, 0.0)
            upd = tn_small(left, aug[0])
            for q in range(p + 2, tiles):
                a[q] = jnp.where(inpanel, 0.0, a[q]) - upd[q * SUB : (q + 1) * SUB]
        rs = lax.rsqrt(dvec)
        u = jnp.where(lane >= off + SUB, aug[0], 0.0)
        for j in range(SUB):
            u = jnp.where((lane == off + j) & (sub <= j), cols[0][j], u)
        us.append(u * rs)
        ts.append(jnp.where(lane < off + SUB, aug[0], 0.0) * rs)
    return us, ts


def finish_kernel(scale, g_ref, x_ref, op_ref, co_ref, basis_ref, s_ref, u_ref, w_ref):
    m = x_ref.shape[1]
    nblk = m // NB
    for i, j, row in block_rows(nblk):
        s_ref[i * NB : (i + 1) * NB, j * NB : (j + 1) * NB] = g_ref[row : row + NB, :]
    u_ref[...] = jnp.zeros((m, m), F32)
    w_ref[...] = jnp.zeros((m, m), F32)
    for b in range(nblk):
        o = b * NB
        e = o + NB
        tiles = [s_ref[o + q * SUB : o + (q + 1) * SUB, o:e] for q in range(NB // SUB)]
        us, ts = factor_block(tiles)
        t = jnp.concatenate(ts, 0)
        u_ref[o:e, o:e] = jnp.concatenate(us, 0)
        w_ref[o:e, o:e] = t
        if e < m:
            r = dot6(t, s_ref[o:e, e:], ((1,), (0,)))
            u_ref[o:e, e:] = r
            for i in range(b + 1, nblk):
                c = i * NB
                ri = r[:, c - e : c - e + NB]
                s_ref[c : c + NB, c:] = s_ref[c : c + NB, c:] - dot6(ri, r[:, c - e :], ((0,), (0,)))
        if b > 0:
            w_ref[o:e, :o] = dot6(t, w_ref[o:e, :o], ((1,), (0,)))
        if e < m:
            w_ref[e:, :e] = w_ref[e:, :e] - dot6(r, w_ref[o:e, :e], ((0,), (0,)))
    w = w_ref[...]
    row = lax.broadcasted_iota(jnp.int32, (m, m), 0)
    shifted = jnp.where(row < m - 1, pltpu.roll(u_ref[...], m - 1, 1), 0.0)
    op = dot6(shifted, w, ((1,), (1,)))
    op_ref[...] = op[: m - 1, : m - 1]
    last = w_ref[m - 8 : m, :]
    co_ref[...] = last * (-1.0 / last[7:8, m - 1 : m])
    basis_ref[...] = dot6(x_ref[...], w, ((1,), (1,))) * scale


def local_gram(x):
    m = x.shape[1]
    nblk = m // NB
    rows = len(block_rows(nblk)) * NB
    return pl.pallas_call(
        gram_kernel,
        out_shape=jax.ShapeDtypeStruct((rows, NB), F32),
        compiler_params=pltpu.CompilerParams(vmem_limit_bytes=40 * 2**20),
        name="gram",
    )(x)


def finish(gram, x, rows_total):
    n, m = x.shape
    op, co, basis = pl.pallas_call(
        functools.partial(finish_kernel, math.sqrt(rows_total)),
        out_shape=(
            jax.ShapeDtypeStruct((m - 1, m - 1), F32),
            jax.ShapeDtypeStruct((8, m), F32),
            jax.ShapeDtypeStruct((n, m), F32),
        ),
        scratch_shapes=[pltpu.VMEM((m, m), F32)] * 3,
        compiler_params=pltpu.CompilerParams(vmem_limit_bytes=48 * 2**20),
        name="factor",
    )(gram, x)
    return op, co[7, : m - 1], basis


def count_of(axis):
    count = 1
    for name in axis if isinstance(axis, tuple) else (axis,):
        count *= lax.axis_size(name)
    return count


def scatter_sum(part, axis):
    n = count_of(axis)
    return lax.all_to_all(part.reshape(n, -1, NB), axis, 0, 0).sum(0)


def swap_sum(part, axis):
    n = count_of(axis)
    return lax.all_to_all(jnp.broadcast_to(part[None], (n,) + part.shape), axis, 0, 0).sum(0)


def body(snapshots):
    part = local_gram(snapshots)
    part = scatter_sum(part, ("z", "c"))
    part = swap_sum(part, "y")
    part = swap_sum(part, "x")
    gram = lax.all_gather(part, ("z", "c"), tiled=True)
    rows_total = snapshots.shape[0] * count_of(("x", "y", "z", "c"))
    return finish(gram, snapshots, rows_total)


def solution(mesh):
    axes = ("x", "y", "z", "c")
    fine = Mesh(mesh.devices.reshape(4, 8, 8, 2), axes)
    return jax.shard_map(
        body,
        mesh=fine,
        in_specs=(P(axes, None),),
        out_specs=(P(), P(), P(axes, None)),
        check_vma=False,
    )
```

time: 1840 us -> 106 us (0.06)
  local copies, waits for them, and re-layouts: 663 us -> 1.84 us
  matrix products: 422 us -> 0 us
  loops' own time: 375 us -> 0 us
  waiting for transfers between devices: 290 us -> 0 us
  blocking collectives: 0 us -> 79.6 us
  other arithmetic: 50.8 us -> 0.07 us
  starting transfers between devices: 27.4 us -> 0 us
  Pallas kernels: 0 us -> 23.6 us
    dynamic_slice x1024 -> x0, local copies, waits for them, and re-layouts: 602 us -> none  [the longest x512 301 us: row_step(): pivot = lax.dynamic_slice_in_dim(row_vals[0], i, 1, 0)[0]]
    dot_general x544 -> x0, matrix products: 422 us -> none  [the longest x543 420 us: exact_dot(): jnp.dot(left_side, right_side, precision=lax.Precision.HIGHEST, preferred...]
    another operation x16 -> x0, loops' own time: 375 us -> none  [the longest x8 365 us: small_cholesky(): lax.fori_loop(0, width_n, column_step, (block, jnp.zeros_like(block)))]
    ppermute x9 -> x0, waiting for transfers between devices: 290 us -> none  [partner_2(): return lax.ppermute(block, axis, route)]
    all_to_all x0 -> x3, blocking collectives: none -> 61.2 us  [the longest x1 31.9 us: scatter_sum(): return lax.all_to_all(part.reshape(n, -1, NB), axis, 0, 0).sum(0)]
    sub x512 -> x0, other arithmetic: 38.5 us -> none  [column_step(): work = work - vector[:, None] * vector[None, :]]
    scatter x24 -> x0, local copies, waits for them, and re-layouts: 29 us -> none  [the longest x8 8.64 us: factor_with_inverse(): inverse = inverse.at[start:stop, start:stop].set(block_inverses[block_id])]
    ppermute x9 -> x0, starting transfers between devices: 27.4 us -> none  [partner_2(): return lax.ppermute(block, axis, route)]
where the time goes in v1:
time: 106 us
  blocking collectives  79.6 us (75%)
  Pallas kernels  23.6 us (22%)
  local copies, waits for them, and re-layouts  1.84 us (2%)
    all_to_all x1, blocking collectives, scatter_sum(): return lax.all_to_all(part.reshape(n, -1, NB), axis, 0, 0).sum(0)  31.9 us
    all_to_all x2, blocking collectives, swap_sum(): lax.all_to_all(jnp.broadcast_to(part[None], (n,) + part.shape), axis, 0, 0)  29.4 us
    pallas_call x1, Pallas kernels, finish(): pl.pallas_call(functools.partial(finish_kernel, math.sqrt(rows_total)), o...  22 us
    all_gather x1, blocking collectives, body(): gram = lax.all_gather(part, ('z', 'c'), tiled=True)  18.4 us

profile of v1, /device:TPU:1, one launch (start us, length us, event | category | flops | bytes accessed | tf_op | source)
XLA Modules:
  0.0 105.8 jit_solution(7758624409160764903)
XLA Ops:
  0.6 0.0 copy-start
  0.6 1.2 %copy-done = f32[512,512]{1,0:T(8,128)S(1)} copy-done((f32[512,512]{1,0:T(8,128)S(1)}, f32[512,512]{1,0:T(8,128)}, u32[]{:S(2)}) %copy-start) | copy-done | bytes 1048600
  1.9 1.6 %gram.1 = f32[1280,128]{1,0:T(8,128)S(1)} custom-call(f32[512,512]{1,0:T(8,128)S(1)} %copy-done), custom_call_target="tpu_custom_call" | custom-call | tf_op jit(solution)/shard_map/gram/pallas_call | solution.py:153
  3.5 31.9 %all_to_all.15 = f32[16,80,128]{2,1,0:T(8,128)S(1)} all-to-all(f32[16,80,128]{2,1,0:T(8,128)S(1)} %bitcast.2), channel_id=1, replica_groups=mesh['x'=4,'y'=8,'z'=8,'c'=2] {'z','c'}, dimensions={0} | all-to-all | bytes 1310720 | tf_op jit(solution)/shard_map/all_to_all | solution.py:186
  35.4 20.4 %all_to_all.16 = f32[8,80,128]{2,1,0:T(8,128)S(1)} all-to-all(f32[8,80,128]{2,1,0:T(8,128)S(1)} %broadcast_in_dim.4), channel_id=1, replica_groups=mesh['x'=4,'y'=8,'z'=8,'c'=2] {'y'}, dimensions={0} | all-to-all | bytes 655360 | tf_op jit(solution)/shard_map/all_to_all | solution.py:191
  55.8 0.0 copy-start.1
  55.9 8.9 %all_to_all.17 = f32[4,80,128]{2,1,0:T(8,128)S(1)} all-to-all(f32[4,80,128]{2,1,0:T(8,128)S(1)} %broadcast_in_dim.5), channel_id=1, replica_groups=mesh['x'=4,'y'=8,'z'=8,'c'=2] {'x'}, dimensions={0} | all-to-all | bytes 327680 | tf_op jit(solution)/shard_map/all_to_all | solution.py:191
  64.8 18.4 %all_gather.3.g_ref = f32[1280,128]{1,0:T(8,128)S(1)} all-gather(f32[80,128]{1,0:T(8,128)S(1)} %reduce_sum.29), channel_id=1, replica_groups=mesh['x'=4,'y'=8,'z'=8,'c'=2] {'z','c'}, dimensions={0}, use_global_device_ids=true | all-gather | bytes 696320 | tf_op jit(solution)/shard_map/all_gather | solution.py:199
  83.2 0.0 copy-done.1
  83.2 22.0 %factor.1 = (f32[511,511]{1,0:T(8,128)}, f32[8,512]{1,0:T(8,128)S(1)}, f32[512,512]{1,0:T(8,128)}) custom-call(f32[1280,128]{1,0:T(8,128)S(1)} %all_gather.3.g_ref, f32[512,512]{1,0:T(8,128)S(1)} %copy-done.1), custom_call_target="tpu_custom_call" | custom-call | tf_op jit(solution)/shard_map/factor/pallas_call | solution.py:163
  105.2 0.6 slice.3
  (5 shorter events, 0.1 us)
Async XLA Ops:
  0.6 1.2 %copy-start = (f32[512,512]{1,0:T(8,128)S(1)}, f32[512,512]{1,0:T(8,128)}, u32[]{:S(2)}) copy-start(f32[512,512]{1,0:T(8,128)} %x_ref.3) | copy-start | bytes 3145732
  55.8 27.4 %copy-start.1 = (f32[512,512]{1,0:T(8,128)S(1)}, f32[512,512]{1,0:T(8,128)}, u32[]{:S(2)}) copy-start(f32[512,512]{1,0:T(8,128)} %x_ref.3) | copy-start | bytes 3145732

commit v2 on v1

v2 whole, which is shorter than its diff:
```python
import functools
import math

import jax
import jax.numpy as jnp
from jax import lax
from jax.experimental import pallas as pl
from jax.experimental.pallas import tpu as pltpu
from jax.sharding import Mesh
from jax.sharding import PartitionSpec as P

F32 = jnp.float32
BF = jnp.bfloat16
NB = 128
SUB = 8


def dot6(x, y, dims):
    return lax.dot_general(
        x, y, (dims, ((), ())), precision=lax.Precision.HIGHEST, preferred_element_type=F32
    )


def halves(nblk):
    every = [(i, j) for i in range(nblk) for j in range(i, nblk)]
    cut = (len(every) + 1) // 2
    return every[:cut], every[cut:]


def half_rows(m, count):
    most = len(halves(m // NB)[0]) * NB
    return -(-most // (count * SUB)) * count * SUB


def gram_kernel(which_ref, x_ref, out_ref):
    for half, blocks in enumerate(halves(x_ref.shape[1] // NB)):

        @pl.when(which_ref[0] == half)
        def _():
            done = 0
            for i in sorted({i for i, _ in blocks}):
                js = [j for k, j in blocks if k == i]
                part = dot6(
                    x_ref[:, i * NB : (i + 1) * NB],
                    x_ref[:, js[0] * NB : (js[-1] + 1) * NB],
                    ((0,), (0,)),
                )
                for n in range(len(js)):
                    out_ref[done : done + NB, :] = part[:, n * NB : (n + 1) * NB]
                    done += NB
            out_ref[done:, :] = jnp.zeros((out_ref.shape[0] - done, NB), F32)


def split3(x):
    a = x.astype(BF)
    rest = x - a.astype(F32)
    b = rest.astype(BF)
    c = (rest - b.astype(F32)).astype(BF)
    return a, b, c


def tn_small(x, y):
    xa, xb, xc = split3(x)
    ya, yb, yc = split3(y)
    left = jnp.concatenate([xa, xa, xb, xb, xa, xc], 0)
    right = jnp.concatenate([ya, yb, ya, yb, yc, ya], 0)
    return lax.dot_general(left, right, (((0,), (0,)), ((), ())), preferred_element_type=F32)


def row_of(x, k):
    return jnp.broadcast_to(x[k : k + 1, :], x.shape)


def lane_of(x, j):
    return jnp.take_along_axis(x, jnp.full(x.shape, j, jnp.int32), axis=1)


def reciprocal(d):
    r = pl.reciprocal(d, approx=True)
    r = r * (2.0 - d * r)
    return r * (2.0 - d * r)


def factor_block(tiles_in, tasks):
    tiles = NB // SUB
    sub = lax.broadcasted_iota(jnp.int32, (SUB, NB), 0)
    lane = lax.broadcasted_iota(jnp.int32, (SUB, NB), 1)
    a = list(tiles_in)
    us, ts = [], []
    for p in range(tiles):
        off = p * SUB
        inpanel = (lane >= off) & (lane < off + SUB)
        rows = [a[p]] + ([a[p + 1]] if p + 1 < tiles else [])
        both = range(len(rows))
        cols = [[lane_of(r, off + j) for j in range(SUB)] for r in rows]
        aug = [jnp.where(inpanel, (lane == off + sub).astype(F32), rows[0])]
        if len(rows) > 1:
            aug.append(jnp.where(inpanel, 0.0, rows[1]))
        dvec = jnp.zeros((SUB, NB), F32)
        rvec = jnp.zeros((SUB, NB), F32)
        for k in range(SUB):
            d = row_of(cols[0][k], k)
            r = reciprocal(d)
            dvec = jnp.where(sub == k, d, dvec)
            rvec = jnp.where(sub == k, r, rvec)
            below = [jnp.where(sub > k, cols[0][k], 0.0)] + [c[k] for c in cols[1:]]
            for j in range(k + 1, SUB):
                b = row_of(cols[0][j], k)
                for q in both:
                    cols[q][j] = cols[q][j] - (below[q] * b) * r
            b = row_of(aug[0], k) * r
            for q in both:
                aug[q] = aug[q] - below[q] * b
        if len(rows) > 1:
            a[p + 1] = aug[1]
        if p + 2 < tiles:
            left = jnp.where(lane >= off + 2 * SUB, aug[0] * rvec, 0.0)
            upd = tn_small(left, aug[0])
            for q in range(p + 2, tiles):
                a[q] = jnp.where(inpanel, 0.0, a[q]) - upd[q * SUB : (q + 1) * SUB]
        rs = lax.rsqrt(dvec)
        u = jnp.where(lane >= off + SUB, aug[0], 0.0)
        for j in range(SUB):
            u = jnp.where((lane == off + j) & (sub <= j), cols[0][j], u)
        us.append(u * rs)
        ts.append(jnp.where(lane < off + SUB, aug[0], 0.0) * rs)
        for _ in range(-(-len(tasks) // (tiles - p))):
            tasks.pop(0)()
    return jnp.concatenate(us, 0), jnp.concatenate(ts, 0)


def finish_kernel(scale, g_ref, x_ref, op_ref, co_ref, basis_ref, s_ref, h_ref, w_ref):
    n, m = x_ref.shape
    nblk = m // NB
    span = [slice(i * NB, (i + 1) * NB) for i in range(nblk)]
    at = {}
    for half, blocks in enumerate(halves(nblk)):
        for k, ij in enumerate(blocks):
            at[ij] = (half, slice(k * NB, (k + 1) * NB))

    def left_over(b, i, j):
        return g_ref[at[i, j]] if b == 0 else s_ref[span[i], span[j]]

    def store_op(i, j, value):
        op_ref[i * NB : min(i * NB + NB, m - 1), j * NB : min(j * NB + NB, m - 1)] = value[
            : min(NB, m - 1 - i * NB), : min(NB, m - 1 - j * NB)
        ]

    def op_block(i, j):
        k = slice(max(0, i - 1) * NB, (j + 1) * NB)
        store_op(i, j, dot6(h_ref[span[i], k], w_ref[span[j], k], ((1,), (1,))))

    def tasks_after(b, u, t, r):
        o, e = b * NB, (b + 1) * NB
        later = range(b + 1, nblk)
        tasks = []

        def panel(j):
            r[j] = dot6(t, left_over(b, b, j), ((1,), (0,)))

        def trail(i, j):
            s_ref[span[i], span[j]] = left_over(b, i, j) - dot6(r[i], r[j], ((0,), (0,)))

        def own_inverse():
            if b > 0:
                w_ref[o:e, :o] = dot6(t, w_ref[o:e, :o], ((1,), (0,)))
            w_ref[o:e, o:e] = t

        def later_inverse(i):
            if b > 0:
                w_ref[span[i], :o] = w_ref[span[i], :o] - dot6(r[i], w_ref[o:e, :o], ((0,), (0,)))
            w_ref[span[i], o:e] = -dot6(r[i], t, ((0,), (0,)))

        def moved():
            pieces = ([jnp.zeros((NB, NB), F32)] if b else []) + [u] + [r[j] for j in later]
            row = jnp.concatenate(pieces, 1)
            h_ref[o:e, m - row.shape[1] :] = pltpu.roll(row, row.shape[1] - 1, 1)

        def basis(c):
            basis_ref[c : c + NB, o:e] = (
                dot6(x_ref[c : c + NB, :e], w_ref[o:e, :e], ((1,), (1,))) * scale
            )

        for j in range(b + 2, nblk):
            tasks.append(functools.partial(panel, j))
        tasks.append(own_inverse)
        for i in later:
            for j in range(max(i, b + 2), nblk):
                tasks.append(functools.partial(trail, i, j))
        for i in later:
            tasks.append(functools.partial(later_inverse, i))
        tasks.append(moved)
        for c in range(0, n, NB):
            tasks.append(functools.partial(basis, c))
        for i in range(b + 1):
            tasks.append(functools.partial(op_block, i, b))
        if b > 0:
            tasks.append(functools.partial(op_block, b, b - 1))
        for i in range(b + 2, nblk):
            tasks.append(functools.partial(store_op, i, b, jnp.zeros((NB, NB), F32)))
        return tasks

    tasks = []
    first = left_over(0, 0, 0)
    for b in range(nblk):
        tiles = [first[q * SUB : (q + 1) * SUB] for q in range(NB // SUB)]
        u, t = factor_block(tiles, tasks)
        r = {}
        if b + 1 < nblk:
            r[b + 1] = dot6(t, left_over(b, b, b + 1), ((1,), (0,)))
            first = left_over(b, b + 1, b + 1) - dot6(r[b + 1], r[b + 1], ((0,), (0,)))
        tasks = tasks_after(b, u, t, r)
    for task in tasks:
        task()
    last = w_ref[m - 8 : m, :]
    co_ref[...] = last * (-1.0 / last[7:8, m - 1 : m])


def local_gram(x, which, count):
    m = x.shape[1]
    return pl.pallas_call(
        gram_kernel,
        out_shape=jax.ShapeDtypeStruct((half_rows(m, count), NB), F32),
        in_specs=[
            pl.BlockSpec(memory_space=pltpu.SMEM),
            pl.BlockSpec(memory_space=pltpu.VMEM),
        ],
        compiler_params=pltpu.CompilerParams(vmem_limit_bytes=40 * 2**20),
        cost_estimate=pl.CostEstimate(
            flops=x.shape[0] * m * m * 4, bytes_accessed=x.size * 6, transcendentals=0
        ),
        name="gram",
    )(which.reshape(1), x)


def finish(gram, x, rows_total):
    n, m = x.shape
    op, co, basis = pl.pallas_call(
        functools.partial(finish_kernel, math.sqrt(rows_total)),
        out_shape=(
            jax.ShapeDtypeStruct((m - 1, m - 1), F32),
            jax.ShapeDtypeStruct((8, m), F32),
            jax.ShapeDtypeStruct((n, m), F32),
        ),
        scratch_shapes=[pltpu.VMEM((m, m), F32)] * 3,
        compiler_params=pltpu.CompilerParams(vmem_limit_bytes=48 * 2**20),
        name="factor",
    )(gram, x)
    return op, co[7, : m - 1], basis


def count_of(axis):
    count = 1
    for name in axis if isinstance(axis, tuple) else (axis,):
        count *= lax.axis_size(name)
    return count


def scatter_sum(part, axis):
    n = count_of(axis)
    return lax.all_to_all(part.reshape(n, -1, NB), axis, 0, 0).sum(0)


def swap(part, axis):
    n = count_of(axis)
    return lax.all_to_all(jnp.broadcast_to(part[None], (n,) + part.shape), axis, 0, 0)


def body(snapshots):
    plane = ("x", "y")
    core = lax.axis_index("c").astype(jnp.int32)
    count = count_of(plane)
    theirs = lax.ppermute(local_gram(snapshots, 1 - core, count), "c", [(0, 1), (1, 0)])
    part = local_gram(snapshots, core, count) + theirs
    part = scatter_sum(part, plane)
    part = swap(part, "z").sum(0)
    part = swap(part, plane).reshape(-1, NB)
    gram = lax.all_gather(part, "c")
    rows_total = snapshots.shape[0] * count_of(("x", "y", "z", "c"))
    return finish(gram, snapshots, rows_total)


def solution(mesh):
    axes = ("x", "y", "z", "c")
    fine = Mesh(mesh.devices.reshape(4, 8, 8, 2), axes)
    return jax.shard_map(
        body,
        mesh=fine,
        in_specs=(P(axes, None),),
        out_specs=(P(), P(), P(axes, None)),
        check_vma=False,
    )
```

time: 106 us -> 92.8 us (0.88)
  blocking collectives: 79.6 us -> 58.4 us
  starting transfers between devices: 0 us -> 8.8 us
  Pallas kernels: 23.6 us -> 22.3 us
    all_to_all x1, blocking collectives: 31.9 us -> 15.9 us  [scatter_sum(): return lax.all_to_all(part.reshape(n, -1, NB), axis, 0, 0).sum(0)]
    all_gather x1, blocking collectives: 18.4 us -> 7.42 us  [body(): gram = lax.all_gather(part, 'c')]
    ppermute x0 -> x1, starting transfers between devices: none -> 8.8 us  [body(): lax.ppermute(local_gram(snapshots, 1 - core, count), 'c', [(0, 1), (1, 0)])]
    all_to_all x2, blocking collectives: 29.4 us -> 35.1 us  [swap(): lax.all_to_all(jnp.broadcast_to(part[None], (n,) + part.shape), axis, 0, 0)]
    pallas_call x1, Pallas kernels: 22 us -> 20.5 us  [finish(): pl.pallas_call(functools.partial(finish_kernel, math.sqrt(rows_total)), o...]
  transfers between devices with their start and end apart: 0 -> 1, of which waited for: 0 -> 1; matrix products, arithmetic and copies ran while one was open for 0% -> 0% of each run, Pallas kernels for 0% -> 1%
where the time goes in v2:
time: 92.8 us; the launch traced here: 92.5 us
  blocking collectives  58.4 us (63%)
  Pallas kernels  22.3 us (24%)
  starting transfers between devices  8.8 us (9%)
  local copies, waits for them, and re-layouts  1.84 us (2%)
    all_to_all x2, blocking collectives, swap(): lax.all_to_all(jnp.broadcast_to(part[None], (n,) + part.shape), axis, 0, 0)  35.1 us
    pallas_call x1, Pallas kernels, finish(): pl.pallas_call(functools.partial(finish_kernel, math.sqrt(rows_total)), o...  20.5 us
    all_to_all x1, blocking collectives, scatter_sum(): return lax.all_to_all(part.reshape(n, -1, NB), axis, 0, 0).sum(0)  15.9 us
    ppermute x1, starting transfers between devices, body(): lax.ppermute(local_gram(snapshots, 1 - core, count), 'c', [(0, 1), (1, 0)])  8.8 us
    all_gather x1, blocking collectives, body(): gram = lax.all_gather(part, 'c')  7.42 us
  transfers between devices with their start and end apart: 1, of which 1 were waited for; matrix products, arithmetic and copies ran while one was open for 0% of the time, Pallas kernels for 1%

profile of v2, /device:TPU:1, one launch (start us, length us, event | category | flops | bytes accessed | tf_op | source)
XLA Modules:
  0.0 92.5 jit_solution(16721797281379530806)
XLA Ops:
  0.6 0.0 copy-start
  0.6 1.2 %copy-done = f32[512,512]{1,0:T(8,128)S(1)} copy-done((f32[512,512]{1,0:T(8,128)S(1)}, f32[512,512]{1,0:T(8,128)}, u32[]{:S(2)}) %copy-start) | copy-done | bytes 1048600
  1.9 0.0 copy-start.1
  1.9 0.9 gram.3
  2.8 8.8 %collective-permute-start = (f32[768,128]{1,0:T(8,128)S(1)}, f32[768,128]{1,0:T(8,128)S(1)}, u32[]{:S(2)}, u32[]{:S(2)}) collective-permute-start(f32[768,128]{1,0:T(8,128)S(1)} %gram.3), channel_id=1, source_target_pairs={{0,1},{1,0},{2,3},{3,2},{4,5},{5,4},{6,7},{7,6},{8,9},{9,8},{10,11... | collective-permute-start | bytes 1179656 | tf_op jit(solution)/shard_map/ppermute | solution.py:273
  11.6 0.0 copy-done.1
  11.6 0.9 gram.2
  12.5 0.4 collective-permute-done
  12.9 15.9 %all_to_all.15 = f32[32,24,128]{2,1,0:T(8,128)S(1)} all-to-all(f32[32,24,128]{2,1,0:T(8,128)S(1)} %bitcast.5), channel_id=1, replica_groups=mesh['x'=4,'y'=8,'z'=8,'c'=2] {'x','y'}, dimensions={0} | all-to-all | bytes 786432 | tf_op jit(solution)/shard_map/all_to_all | solution.py:261
  28.9 17.4 %all_to_all.16 = f32[8,24,128]{2,1,0:T(8,128)S(1)} all-to-all(f32[8,24,128]{2,1,0:T(8,128)S(1)} %broadcast_in_dim.4), channel_id=1, replica_groups=mesh['x'=4,'y'=8,'z'=8,'c'=2] {'z'}, dimensions={0} | all-to-all | bytes 196608 | tf_op jit(solution)/shard_map/all_to_all | solution.py:266
  46.3 17.7 %all_to_all.17 = f32[32,24,128]{2,1,0:T(8,128)S(1)} all-to-all(f32[32,24,128]{2,1,0:T(8,128)S(1)} %broadcast_in_dim.5), channel_id=1, replica_groups=mesh['x'=4,'y'=8,'z'=8,'c'=2] {'x','y'}, dimensions={0} | all-to-all | bytes 786432 | tf_op jit(solution)/shard_map/all_to_all | solution.py:266
  64.0 7.4 %all_gather.3.g_ref = f32[2,768,128]{2,1,0:T(8,128)S(1)} all-gather(f32[1,768,128]{2,1,0:T(8,128)S(1)} %bitcast.6), channel_id=1, replica_groups=mesh['x'=4,'y'=8,'z'=8,'c'=2] {'c'}, dimensions={0}, use_global_device_ids=true | all-gather | bytes 1179648 | tf_op jit(solution)/shard_map/all_gather | solution.py:278
  71.5 20.5 %factor.1 = (f32[511,511]{1,0:T(8,128)}, f32[8,512]{1,0:T(8,128)S(1)}, f32[512,512]{1,0:T(8,128)}) custom-call(f32[2,768,128]{2,1,0:T(8,128)S(1)} %all_gather.3.g_ref, f32[512,512]{1,0:T(8,128)S(1)} %copy-done.1), custom_call_target="tpu_custom_call" | custom-call | tf_op jit(solution)/shard_map/factor/pallas_call | solution.py:238
  91.9 0.6 slice.3
  (5 shorter events, 0.1 us)
Async XLA Ops:
  0.6 1.2 %copy-start = (f32[512,512]{1,0:T(8,128)S(1)}, f32[512,512]{1,0:T(8,128)}, u32[]{:S(2)}) copy-start(f32[512,512]{1,0:T(8,128)} %x_ref.5) | copy-start | bytes 3145732
  1.9 9.7 %copy-start.1 = (f32[512,512]{1,0:T(8,128)S(1)}, f32[512,512]{1,0:T(8,128)}, u32[]{:S(2)}) copy-start(f32[512,512]{1,0:T(8,128)} %x_ref.5) | copy-start | bytes 3145732
  2.8 10.1 %collective-permute-start = (f32[768,128]{1,0:T(8,128)S(1)}, f32[768,128]{1,0:T(8,128)S(1)}, u32[]{:S(2)}, u32[]{:S(2)}) collective-permute-start(f32[768,128]{1,0:T(8,128)S(1)} %gram.3), channel_id=1, source_target_pairs={{0,1},{1,0},{2,3},{3,2},{4,5},{5,4},{6,7},{7,6},{8,9},{9,8},{10,11... | collective-permute-start | bytes 1179656 | tf_op jit(solution)/shard_map/ppermute | solution.py:273

commit v3 on v2

--- a/solution.py
+++ b/solution.py
@@ -13,11 +13,19 @@
 BF = jnp.bfloat16
 NB = 128
 SUB = 8
+WT = 2
+LT = 2
 
 
 def dot6(x, y, dims):
     return lax.dot_general(
         x, y, (dims, ((), ())), precision=lax.Precision.HIGHEST, preferred_element_type=F32
+    )
+
+
+def dot_high(x, y):
+    return lax.dot_general(
+        x, y, (((1,), (1,)), ((), ())), precision=lax.Precision.HIGH, preferred_element_type=F32
     )
 
 
@@ -75,61 +83,61 @@
     return jnp.take_along_axis(x, jnp.full(x.shape, j, jnp.int32), axis=1)
 
 
-def reciprocal(d):
-    r = pl.reciprocal(d, approx=True)
-    r = r * (2.0 - d * r)
-    return r * (2.0 - d * r)
-
-
 def factor_block(tiles_in, tasks):
     tiles = NB // SUB
     sub = lax.broadcasted_iota(jnp.int32, (SUB, NB), 0)
     lane = lax.broadcasted_iota(jnp.int32, (SUB, NB), 1)
     a = list(tiles_in)
     us, ts = [], []
-    for p in range(tiles):
+    for p in range(0, tiles, WT):
         off = p * SUB
-        inpanel = (lane >= off) & (lane < off + SUB)
-        rows = [a[p]] + ([a[p + 1]] if p + 1 < tiles else [])
-        both = range(len(rows))
-        cols = [[lane_of(r, off + j) for j in range(SUB)] for r in rows]
-        aug = [jnp.where(inpanel, (lane == off + sub).astype(F32), rows[0])]
-        if len(rows) > 1:
-            aug.append(jnp.where(inpanel, 0.0, rows[1]))
-        dvec = jnp.zeros((SUB, NB), F32)
-        rvec = jnp.zeros((SUB, NB), F32)
-        for k in range(SUB):
-            d = row_of(cols[0][k], k)
-            r = reciprocal(d)
-            dvec = jnp.where(sub == k, d, dvec)
-            rvec = jnp.where(sub == k, r, rvec)
-            below = [jnp.where(sub > k, cols[0][k], 0.0)] + [c[k] for c in cols[1:]]
-            for j in range(k + 1, SUB):
-                b = row_of(cols[0][j], k)
-                for q in both:
-                    cols[q][j] = cols[q][j] - (below[q] * b) * r
-            b = row_of(aug[0], k) * r
-            for q in both:
-                aug[q] = aug[q] - below[q] * b
-        if len(rows) > 1:
-            a[p + 1] = aug[1]
-        if p + 2 < tiles:
-            left = jnp.where(lane >= off + 2 * SUB, aug[0] * rvec, 0.0)
-            upd = tn_small(left, aug[0])
-            for q in range(p + 2, tiles):
-                a[q] = jnp.where(inpanel, 0.0, a[q]) - upd[q * SUB : (q + 1) * SUB]
-        rs = lax.rsqrt(dvec)
-        u = jnp.where(lane >= off + SUB, aug[0], 0.0)
-        for j in range(SUB):
-            u = jnp.where((lane == off + j) & (sub <= j), cols[0][j], u)
-        us.append(u * rs)
-        ts.append(jnp.where(lane < off + SUB, aug[0], 0.0) * rs)
-        for _ in range(-(-len(tasks) // (tiles - p))):
+        wide = WT * SUB
+        inside = (lane >= off) & (lane < off + wide)
+        reach = range(min(WT + LT, tiles - p))
+        cols = [[lane_of(a[p + q], off + j) for j in range(wide)] for q in reach]
+        unit = [(lane == off + q * SUB + sub).astype(F32) if q < WT else 0.0 for q in reach]
+        aug = [jnp.where(inside, unit[q], a[p + q]) for q in reach]
+        dvec = [jnp.zeros((SUB, NB), F32) for _ in range(WT)]
+        rvec = [jnp.zeros((SUB, NB), F32) for _ in range(WT)]
+        for step in range(wide):
+            t, k = divmod(step, SUB)
+            d = row_of(cols[t][step], k)
+            r = pl.reciprocal(d, approx=True)
+            dvec[t] = jnp.where(sub == k, d, dvec[t])
+            rvec[t] = jnp.where(sub == k, r, rvec[t])
+            own = jnp.where(sub > k, cols[t][step], 0.0)
+            below = {q: own if q == t else cols[q][step] * r for q in reach if q >= t}
+            for j in range(step + 1, wide):
+                b = row_of(cols[t][j], k)
+                for q in below:
+                    if q == t:
+                        cols[q][j] = cols[q][j] - (own * b) * r
+                    else:
+                        cols[q][j] = cols[q][j] - below[q] * b
+            b = row_of(aug[t], k)
+            for q in below:
+                aug[q] = aug[q] - (own * (b * r) if q == t else below[q] * b)
+        for q in reach[WT:]:
+            a[p + q] = aug[q]
+        lo = off + len(reach) * SUB
+        if lo < NB:
+            left = [jnp.where(lane >= lo, aug[q] * rvec[q], 0.0) for q in range(WT)]
+            upd = tn_small(jnp.concatenate(left, 0), jnp.concatenate(aug[:WT], 0))
+            for q in range(p + len(reach), tiles):
+                a[q] = jnp.where(inside, 0.0, a[q]) - upd[q * SUB : (q + 1) * SUB]
+        for q in range(WT):
+            rs = lax.rsqrt(dvec[q])
+            u = jnp.where(lane >= off + wide, aug[q], 0.0)
+            for j in range(q * SUB, wide):
+                u = jnp.where((lane == off + j) & (sub <= j - q * SUB), cols[q][j], u)
+            us.append(u * rs)
+            ts.append(jnp.where(lane < off + wide, aug[q], 0.0) * rs)
+        for _ in range(-(-len(tasks) // ((tiles - p) // WT))):
             tasks.pop(0)()
     return jnp.concatenate(us, 0), jnp.concatenate(ts, 0)
 
 
-def finish_kernel(scale, g_ref, x_ref, op_ref, co_ref, basis_ref, s_ref, h_ref, w_ref):
+def finish_kernel(scale, g_ref, x_ref, op_ref, co_ref, basis_ref, s_ref, h_ref, w_ref, y_ref, z_ref):
     n, m = x_ref.shape
     nblk = m // NB
     span = [slice(i * NB, (i + 1) * NB) for i in range(nblk)]
@@ -177,9 +185,25 @@
             h_ref[o:e, m - row.shape[1] :] = pltpu.roll(row, row.shape[1] - 1, 1)
 
         def basis(c):
-            basis_ref[c : c + NB, o:e] = (
-                dot6(x_ref[c : c + NB, :e], w_ref[o:e, :e], ((1,), (1,))) * scale
+            if b + 1 < nblk:
+                part = dot_high(x_ref[c : c + NB, :e], w_ref[o:e, :e])
+            else:
+                part = dot_high(y_ref[c : c + NB, :], t)
+            basis_ref[c : c + NB, o:e] = part * scale
+
+        def basis_ahead(c):
+            y_ref[c : c + NB, :] = x_ref[c : c + NB, e:] + dot_high(
+                x_ref[c : c + NB, :e], w_ref[e:, :e]
             )
+
+        def op_ahead(i):
+            k = slice(max(0, i - 1) * NB, e)
+            z_ref[span[i], :] = h_ref[span[i], e:] + dot6(
+                h_ref[span[i], k], w_ref[e:, k], ((1,), (1,))
+            )
+
+        def op_last(i):
+            store_op(i, b, dot6(z_ref[span[i], :], t, ((1,), (1,))))
 
         for j in range(b + 2, nblk):
             tasks.append(functools.partial(panel, j))
@@ -193,7 +217,15 @@
         for c in range(0, n, NB):
             tasks.append(functools.partial(basis, c))
         for i in range(b + 1):
-            tasks.append(functools.partial(op_block, i, b))
+            if b + 1 < nblk or i == b:
+                tasks.append(functools.partial(op_block, i, b))
+            else:
+                tasks.append(functools.partial(op_last, i))
+        if b + 2 == nblk:
+            for c in range(0, n, NB):
+                tasks.append(functools.partial(basis_ahead, c))
+            for i in range(b + 1):
+                tasks.append(functools.partial(op_ahead, i))
         if b > 0:
             tasks.append(functools.partial(op_block, b, b - 1))
         for i in range(b + 2, nblk):
@@ -242,7 +274,8 @@
             jax.ShapeDtypeStruct((8, m), F32),
             jax.ShapeDtypeStruct((n, m), F32),
         ),
-        scratch_shapes=[pltpu.VMEM((m, m), F32)] * 3,
+        scratch_shapes=[pltpu.VMEM((m, m), F32)] * 3
+        + [pltpu.VMEM((n, NB), F32), pltpu.VMEM((m - NB, NB), F32)],
         compiler_params=pltpu.CompilerParams(vmem_limit_bytes=48 * 2**20),
         name="factor",
     )(gram, x)

time: 92.8 us -> 86.5 us (0.932)
  Pallas kernels: 22.3 us -> 16 us
    pallas_call x1, Pallas kernels: 20.5 us -> 14.2 us  [finish(): pl.pallas_call(functools.partial(finish_kernel, math.sqrt(rows_total)), o...]
where the time goes in v3:
time: 86.5 us; the launch traced here: 86.2 us
  blocking collectives  58.4 us (68%)
  Pallas kernels  16 us (18%)
  starting transfers between devices  8.8 us (10%)
  local copies, waits for them, and re-layouts  1.84 us (2%)
    all_to_all x2, blocking collectives, swap(): lax.all_to_all(jnp.broadcast_to(part[None], (n,) + part.shape), axis, 0, 0)  35.1 us
    all_to_all x1, blocking collectives, scatter_sum(): return lax.all_to_all(part.reshape(n, -1, NB), axis, 0, 0).sum(0)  15.9 us
    pallas_call x1, Pallas kernels, finish(): pl.pallas_call(functools.partial(finish_kernel, math.sqrt(rows_total)), o...  14.2 us
    ppermute x1, starting transfers between devices, body(): lax.ppermute(local_gram(snapshots, 1 - core, count), 'c', [(0, 1), (1, 0)])  8.8 us
    all_gather x1, blocking collectives, body(): gram = lax.all_gather(part, 'c')  7.42 us
    pallas_call x2, Pallas kernels, local_gram(): pl.pallas_call(gram_kernel, out_shape=jax.ShapeDtypeStruct((half_rows(m,...  1.81 us
  transfers between devices with their start and end apart: 1, of which 1 were waited for; matrix products, arithmetic and copies ran while one was open for 0% of the time, Pallas kernels for 1%

profile of v3, /device:TPU:1, one launch (start us, length us, event | category | flops | bytes accessed | tf_op | source)
XLA Modules:
  0.0 86.2 jit_solution(11195446610488900298)
XLA Ops:
  0.6 0.0 copy-start
  0.6 1.2 %copy-done = f32[512,512]{1,0:T(8,128)S(1)} copy-done((f32[512,512]{1,0:T(8,128)S(1)}, f32[512,512]{1,0:T(8,128)}, u32[]{:S(2)}) %copy-start) | copy-done | bytes 1048600
  1.9 0.0 copy-start.1
  1.9 0.9 %gram.3 = f32[768,128]{1,0:T(8,128)S(1)} custom-call(s32[1]{0:T(128)} %bitcast.1.which_ref, f32[512,512]{1,0:T(8,128)S(1)} %copy-done), custom_call_target="tpu_custom_call" | custom-call | flops 536870912 | bytes 1572864 | tf_op jit(solution)/shard_map/gram/pallas_call | solution.py:253
  2.8 8.8 %collective-permute-start = (f32[768,128]{1,0:T(8,128)S(1)}, f32[768,128]{1,0:T(8,128)S(1)}, u32[]{:S(2)}, u32[]{:S(2)}) collective-permute-start(f32[768,128]{1,0:T(8,128)S(1)} %gram.3), channel_id=1, source_target_pairs={{0,1},{1,0},{2,3},{3,2},{4,5},{5,4},{6,7},{7,6},{8,9},{9,8},{10,11... | collective-permute-start | bytes 1179656 | tf_op jit(solution)/shard_map/ppermute | solution.py:306
  11.6 0.0 copy-done.1
  11.6 0.9 %gram.2 = f32[768,128]{1,0:T(8,128)S(1)} custom-call(s32[1]{0:T(128)} %bitcast.which_ref, f32[512,512]{1,0:T(8,128)S(1)} %copy-done.1), custom_call_target="tpu_custom_call" | custom-call | flops 536870912 | bytes 1572864 | tf_op jit(solution)/shard_map/gram/pallas_call | solution.py:253
  12.5 0.4 collective-permute-done
  12.9 15.9 %all_to_all.15 = f32[32,24,128]{2,1,0:T(8,128)S(1)} all-to-all(f32[32,24,128]{2,1,0:T(8,128)S(1)} %bitcast.5), channel_id=1, replica_groups=mesh['x'=4,'y'=8,'z'=8,'c'=2] {'x','y'}, dimensions={0} | all-to-all | bytes 786432 | tf_op jit(solution)/shard_map/all_to_all | solution.py:294
  28.9 17.4 %all_to_all.16 = f32[8,24,128]{2,1,0:T(8,128)S(1)} all-to-all(f32[8,24,128]{2,1,0:T(8,128)S(1)} %broadcast_in_dim.4), channel_id=1, replica_groups=mesh['x'=4,'y'=8,'z'=8,'c'=2] {'z'}, dimensions={0} | all-to-all | bytes 196608 | tf_op jit(solution)/shard_map/all_to_all | solution.py:299
  46.3 17.7 %all_to_all.17 = f32[32,24,128]{2,1,0:T(8,128)S(1)} all-to-all(f32[32,24,128]{2,1,0:T(8,128)S(1)} %broadcast_in_dim.5), channel_id=1, replica_groups=mesh['x'=4,'y'=8,'z'=8,'c'=2] {'x','y'}, dimensions={0} | all-to-all | bytes 786432 | tf_op jit(solution)/shard_map/all_to_all | solution.py:299
  64.0 7.4 %all_gather.3.g_ref = f32[2,768,128]{2,1,0:T(8,128)S(1)} all-gather(f32[1,768,128]{2,1,0:T(8,128)S(1)} %bitcast.6), channel_id=1, replica_groups=mesh['x'=4,'y'=8,'z'=8,'c'=2] {'c'}, dimensions={0}, use_global_device_ids=true | all-gather | bytes 1179648 | tf_op jit(solution)/shard_map/all_gather | solution.py:311
  71.5 14.2 %factor.1 = (f32[511,511]{1,0:T(8,128)}, f32[8,512]{1,0:T(8,128)S(1)}, f32[512,512]{1,0:T(8,128)}) custom-call(f32[2,768,128]{2,1,0:T(8,128)S(1)} %all_gather.3.g_ref, f32[512,512]{1,0:T(8,128)S(1)} %copy-done.1), custom_call_target="tpu_custom_call" | custom-call | tf_op jit(solution)/shard_map/factor/pallas_call | solution.py:270
  85.7 0.6 slice.3
  (5 shorter events, 0.1 us)
Async XLA Ops:
  0.6 1.2 %copy-start = (f32[512,512]{1,0:T(8,128)S(1)}, f32[512,512]{1,0:T(8,128)}, u32[]{:S(2)}) copy-start(f32[512,512]{1,0:T(8,128)} %x_ref.5) | copy-start | bytes 3145732
  1.9 9.7 %copy-start.1 = (f32[512,512]{1,0:T(8,128)S(1)}, f32[512,512]{1,0:T(8,128)}, u32[]{:S(2)}) copy-start(f32[512,512]{1,0:T(8,128)} %x_ref.5) | copy-start | bytes 3145732
  2.8 10.1 %collective-permute-start = (f32[768,128]{1,0:T(8,128)S(1)}, f32[768,128]{1,0:T(8,128)S(1)}, u32[]{:S(2)}, u32[]{:S(2)}) collective-permute-start(f32[768,128]{1,0:T(8,128)S(1)} %gram.3), channel_id=1, source_target_pairs={{0,1},{1,0},{2,3},{3,2},{4,5},{5,4},{6,7},{7,6},{8,9},{9,8},{10,11... | collective-permute-start | bytes 1179656 | tf_op jit(solution)/shard_map/ppermute | solution.py:306

commit v4 on v3

--- a/solution.py
+++ b/solution.py
@@ -13,6 +13,7 @@
 BF = jnp.bfloat16
 NB = 128
 SUB = 8
+ROWS = 4
 WT = 2
 LT = 2
 
@@ -37,7 +38,7 @@
 
 def half_rows(m, count):
     most = len(halves(m // NB)[0]) * NB
-    return -(-most // (count * SUB)) * count * SUB
+    return -(-most // (count * ROWS)) * count * ROWS
 
 
 def gram_kernel(which_ref, x_ref, out_ref):
@@ -56,23 +57,8 @@
                 for n in range(len(js)):
                     out_ref[done : done + NB, :] = part[:, n * NB : (n + 1) * NB]
                     done += NB
-            out_ref[done:, :] = jnp.zeros((out_ref.shape[0] - done, NB), F32)
-
-
-def split3(x):
-    a = x.astype(BF)
-    rest = x - a.astype(F32)
-    b = rest.astype(BF)
-    c = (rest - b.astype(F32)).astype(BF)
-    return a, b, c
-
-
-def tn_small(x, y):
-    xa, xb, xc = split3(x)
-    ya, yb, yc = split3(y)
-    left = jnp.concatenate([xa, xa, xb, xb, xa, xc], 0)
-    right = jnp.concatenate([ya, yb, ya, yb, yc, ya], 0)
-    return lax.dot_general(left, right, (((0,), (0,)), ((), ())), preferred_element_type=F32)
+            if done < out_ref.shape[0]:
+                out_ref[done:, :] = jnp.zeros((out_ref.shape[0] - done, NB), F32)
 
 
 def row_of(x, k):
@@ -85,56 +71,58 @@
 
 def factor_block(tiles_in, tasks):
     tiles = NB // SUB
+    wide = WT * SUB
     sub = lax.broadcasted_iota(jnp.int32, (SUB, NB), 0)
     lane = lax.broadcasted_iota(jnp.int32, (SUB, NB), 1)
+    at_row = [sub == k for k in range(SUB)]
     a = list(tiles_in)
-    us, ts = [], []
+    ts = []
     for p in range(0, tiles, WT):
         off = p * SUB
-        wide = WT * SUB
+        own = range(WT)
         inside = (lane >= off) & (lane < off + wide)
-        reach = range(min(WT + LT, tiles - p))
-        cols = [[lane_of(a[p + q], off + j) for j in range(wide)] for q in reach]
-        unit = [(lane == off + q * SUB + sub).astype(F32) if q < WT else 0.0 for q in reach]
-        aug = [jnp.where(inside, unit[q], a[p + q]) for q in reach]
-        dvec = [jnp.zeros((SUB, NB), F32) for _ in range(WT)]
-        rvec = [jnp.zeros((SUB, NB), F32) for _ in range(WT)]
+        near = range(p + WT, min(p + WT + LT, tiles))
+        far = range(min(p + WT + LT, tiles), tiles)
+        cols = [[lane_of(a[p + q], off + j) for j in range(wide)] for q in own]
+        near_cols = [[lane_of(a[q], off + j) for j in range(wide)] for q in near]
+        full = [jnp.where(inside, (lane == off + q * SUB + sub).astype(F32), a[p + q]) for q in own]
+        forward = [jnp.zeros((SUB, NB), F32) for _ in own]
+        dvec = [jnp.ones((SUB, NB), F32) for _ in own]
         for step in range(wide):
             t, k = divmod(step, SUB)
             d = row_of(cols[t][step], k)
             r = pl.reciprocal(d, approx=True)
-            dvec[t] = jnp.where(sub == k, d, dvec[t])
-            rvec[t] = jnp.where(sub == k, r, rvec[t])
-            own = jnp.where(sub > k, cols[t][step], 0.0)
-            below = {q: own if q == t else cols[q][step] * r for q in reach if q >= t}
+            forward[t] = jnp.where(at_row[k], full[t], forward[t])
+            dvec[t] = jnp.where(at_row[k], d, dvec[t])
+            mult = [jnp.where(at_row[k], 0.0, cols[q][step]) * r if q == t else cols[q][step] * r for q in own]
             for j in range(step + 1, wide):
                 b = row_of(cols[t][j], k)
-                for q in below:
-                    if q == t:
-                        cols[q][j] = cols[q][j] - (own * b) * r
-                    else:
-                        cols[q][j] = cols[q][j] - below[q] * b
-            b = row_of(aug[t], k)
-            for q in below:
-                aug[q] = aug[q] - (own * (b * r) if q == t else below[q] * b)
-        for q in reach[WT:]:
-            a[p + q] = aug[q]
-        lo = off + len(reach) * SUB
-        if lo < NB:
-            left = [jnp.where(lane >= lo, aug[q] * rvec[q], 0.0) for q in range(WT)]
-            upd = tn_small(jnp.concatenate(left, 0), jnp.concatenate(aug[:WT], 0))
-            for q in range(p + len(reach), tiles):
-                a[q] = jnp.where(inside, 0.0, a[q]) - upd[q * SUB : (q + 1) * SUB]
-        for q in range(WT):
-            rs = lax.rsqrt(dvec[q])
-            u = jnp.where(lane >= off + wide, aug[q], 0.0)
-            for j in range(q * SUB, wide):
-                u = jnp.where((lane == off + j) & (sub <= j - q * SUB), cols[q][j], u)
-            us.append(u * rs)
-            ts.append(jnp.where(lane < off + wide, aug[q], 0.0) * rs)
+                for q in own:
+                    cols[q][j] = cols[q][j] - mult[q] * b
+            b = row_of(full[t], k)
+            for q in own:
+                full[q] = full[q] - mult[q] * b
+        worth = [full[q] * pl.reciprocal(dvec[q], approx=True) for q in own]
+        sums = [jnp.where(inside, 0.0, a[q]) for q in near]
+        for step in range(wide):
+            t, k = divmod(step, SUB)
+            b = row_of(worth[t], k)
+            for q in range(len(near)):
+                sums[q] = sums[q] - near_cols[q][step] * b
+        if len(far):
+            left = jnp.concatenate([jnp.where(inside, a[q], 0.0) for q in far], 0)
+            zeros = [jnp.zeros((n, NB), F32) for n in (off, NB - off - wide)]
+            right = jnp.concatenate([z for z in (zeros[0], *worth, zeros[1]) if z.shape[0]], 0)
+            upd = dot6(left, right, ((1,), (0,)))
+            for n, q in enumerate(far):
+                a[q] = jnp.where(inside, 0.0, a[q]) - upd[n * SUB : (n + 1) * SUB]
+        for n, q in enumerate(near):
+            a[q] = sums[n]
+        for q in own:
+            ts.append(jnp.where(lane < off + wide, forward[q], 0.0) * lax.rsqrt(dvec[q]))
         for _ in range(-(-len(tasks) // ((tiles - p) // WT))):
             tasks.pop(0)()
-    return jnp.concatenate(us, 0), jnp.concatenate(ts, 0)
+    return jnp.concatenate(ts, 0)
 
 
 def finish_kernel(scale, g_ref, x_ref, op_ref, co_ref, basis_ref, s_ref, h_ref, w_ref, y_ref, z_ref):
@@ -158,7 +146,7 @@
         k = slice(max(0, i - 1) * NB, (j + 1) * NB)
         store_op(i, j, dot6(h_ref[span[i], k], w_ref[span[j], k], ((1,), (1,))))
 
-    def tasks_after(b, u, t, r):
+    def tasks_after(b, t, r):
         o, e = b * NB, (b + 1) * NB
         later = range(b + 1, nblk)
         tasks = []
@@ -180,6 +168,9 @@
             w_ref[span[i], o:e] = -dot6(r[i], t, ((0,), (0,)))
 
         def moved():
+            row = lax.broadcasted_iota(jnp.int32, (NB, NB), 0)
+            col = lax.broadcasted_iota(jnp.int32, (NB, NB), 1)
+            u = jnp.where(col >= row, dot6(t, left_over(b, b, b), ((1,), (0,))), 0.0)
             pieces = ([jnp.zeros((NB, NB), F32)] if b else []) + [u] + [r[j] for j in later]
             row = jnp.concatenate(pieces, 1)
             h_ref[o:e, m - row.shape[1] :] = pltpu.roll(row, row.shape[1] - 1, 1)
@@ -236,16 +227,17 @@
     first = left_over(0, 0, 0)
     for b in range(nblk):
         tiles = [first[q * SUB : (q + 1) * SUB] for q in range(NB // SUB)]
-        u, t = factor_block(tiles, tasks)
+        t = factor_block(tiles, tasks)
         r = {}
         if b + 1 < nblk:
             r[b + 1] = dot6(t, left_over(b, b, b + 1), ((1,), (0,)))
             first = left_over(b, b + 1, b + 1) - dot6(r[b + 1], r[b + 1], ((0,), (0,)))
-        tasks = tasks_after(b, u, t, r)
+            s_ref[span[b + 1], span[b + 1]] = first
+        tasks = tasks_after(b, t, r)
     for task in tasks:
         task()
     last = w_ref[m - 8 : m, :]
-    co_ref[...] = last * (-1.0 / last[7:8, m - 1 : m])
+    co_ref[...] = (last * (-1.0 / last[7:8, m - 1 : m]))[7, : m - 1]
 
 
 def local_gram(x, which, count):
@@ -271,7 +263,7 @@
         functools.partial(finish_kernel, math.sqrt(rows_total)),
         out_shape=(
             jax.ShapeDtypeStruct((m - 1, m - 1), F32),
-            jax.ShapeDtypeStruct((8, m), F32),
+            jax.ShapeDtypeStruct((m - 1,), F32),
             jax.ShapeDtypeStruct((n, m), F32),
         ),
         scratch_shapes=[pltpu.VMEM((m, m), F32)] * 3
@@ -279,7 +271,7 @@
         compiler_params=pltpu.CompilerParams(vmem_limit_bytes=48 * 2**20),
         name="factor",
     )(gram, x)
-    return op, co[7, : m - 1], basis
+    return op, co, basis
 
 
 def count_of(axis):
@@ -291,7 +283,7 @@
 
 def scatter_sum(part, axis):
     n = count_of(axis)
-    return lax.all_to_all(part.reshape(n, -1, NB), axis, 0, 0).sum(0)
+    return lax.all_to_all(part.reshape(n, -1, ROWS, NB), axis, 0, 0).sum(0)
 
 
 def swap(part, axis):

time: 86.5 us -> 82.8 us (0.957)
  blocking collectives: 58.4 us -> 55.7 us
    all_to_all x1, blocking collectives: 15.9 us -> 14.6 us  [scatter_sum(): return lax.all_to_all(part.reshape(n, -1, ROWS, NB), axis, 0, 0).sum(0)]
    all_gather x1, blocking collectives: 7.42 us -> 6.48 us  [body(): gram = lax.all_gather(part, 'c')]
where the time goes in v4:
time: 82.8 us; the launch traced here: 82.5 us
  blocking collectives  55.7 us (67%)
  Pallas kernels  15.7 us (19%)
  starting transfers between devices  8.8 us (11%)
  local copies, waits for them, and re-layouts  1.28 us (2%)
    all_to_all x2, blocking collectives, swap(): lax.all_to_all(jnp.broadcast_to(part[None], (n,) + part.shape), axis, 0, 0)  34.6 us
    all_to_all x1, blocking collectives, scatter_sum(): return lax.all_to_all(part.reshape(n, -1, ROWS, NB), axis, 0, 0).sum(0)  14.6 us
    pallas_call x1, Pallas kernels, finish(): pl.pallas_call(functools.partial(finish_kernel, math.sqrt(rows_total)), o...  13.9 us
    ppermute x1, starting transfers between devices, body(): lax.ppermute(local_gram(snapshots, 1 - core, count), 'c', [(0, 1), (1, 0)])  8.8 us
    all_gather x1, blocking collectives, body(): gram = lax.all_gather(part, 'c')  6.48 us
    pallas_call x2, Pallas kernels, local_gram(): pl.pallas_call(gram_kernel, out_shape=jax.ShapeDtypeStruct((half_rows(m,...  1.81 us
  transfers between devices with their start and end apart: 1, of which 1 were waited for; matrix products, arithmetic and copies ran while one was open for 0% of the time, Pallas kernels for 1%

profile of v4, /device:TPU:1, one launch (start us, length us, event | category | flops | bytes accessed | tf_op | source)
XLA Modules:
  0.0 82.5 jit_solution(1382668380892754816)
XLA Ops:
  0.6 0.0 copy-start
  0.6 1.2 %copy-done = f32[512,512]{1,0:T(8,128)S(1)} copy-done((f32[512,512]{1,0:T(8,128)S(1)}, f32[512,512]{1,0:T(8,128)}, u32[]{:S(2)}) %copy-start) | copy-done | bytes 1048600
  1.9 0.0 copy-start.1
  1.9 0.9 %gram.3 = f32[640,128]{1,0:T(8,128)S(1)} custom-call(s32[1]{0:T(128)} %bitcast.1.which_ref, f32[512,512]{1,0:T(8,128)S(1)} %copy-done), custom_call_target="tpu_custom_call" | custom-call | flops 536870912 | bytes 1572864 | tf_op jit(solution)/shard_map/gram/pallas_call | solution.py:245
  2.8 8.8 %collective-permute-start = (f32[640,128]{1,0:T(8,128)S(1)}, f32[640,128]{1,0:T(8,128)S(1)}, u32[]{:S(2)}, u32[]{:S(2)}) collective-permute-start(f32[640,128]{1,0:T(8,128)S(1)} %gram.3), channel_id=1, source_target_pairs={{0,1},{1,0},{2,3},{3,2},{4,5},{5,4},{6,7},{7,6},{8,9},{9,8},{10,11... | collective-permute-start | bytes 983048 | tf_op jit(solution)/shard_map/ppermute | solution.py:298
  11.6 0.0 copy-done.1
  11.6 0.9 %gram.2 = f32[640,128]{1,0:T(8,128)S(1)} custom-call(s32[1]{0:T(128)} %bitcast.which_ref, f32[512,512]{1,0:T(8,128)S(1)} %copy-done.1), custom_call_target="tpu_custom_call" | custom-call | flops 536870912 | bytes 1572864 | tf_op jit(solution)/shard_map/gram/pallas_call | solution.py:245
  12.5 0.3 collective-permute-done
  12.8 14.6 %all_to_all.15 = f32[32,5,4,128]{3,2,1,0:T(4,128)S(1)} all-to-all(f32[32,5,4,128]{3,2,1,0:T(4,128)S(1)} %bitcast.4), channel_id=1, replica_groups=mesh['x'=4,'y'=8,'z'=8,'c'=2] {'x','y'}, dimensions={0} | all-to-all | bytes 655360 | tf_op jit(solution)/shard_map/all_to_all | solution.py:286
  27.4 0.1 reduce_sum.18
  27.5 17.2 %all_to_all.16 = f32[8,5,4,128]{3,2,1,0:T(4,128)S(1)} all-to-all(f32[8,5,4,128]{3,2,1,0:T(4,128)S(1)} %broadcast_in_dim.4), channel_id=1, replica_groups=mesh['x'=4,'y'=8,'z'=8,'c'=2] {'z'}, dimensions={0} | all-to-all | bytes 163840 | tf_op jit(solution)/shard_map/all_to_all | solution.py:291
  44.8 17.4 %all_to_all.17 = f32[32,5,4,128]{3,2,1,0:T(4,128)S(1)} all-to-all(f32[32,5,4,128]{3,2,1,0:T(4,128)S(1)} %broadcast_in_dim.5), channel_id=1, replica_groups=mesh['x'=4,'y'=8,'z'=8,'c'=2] {'x','y'}, dimensions={0} | all-to-all | bytes 655360 | tf_op jit(solution)/shard_map/all_to_all | solution.py:291
  62.2 6.5 %all_gather.3.g_ref = f32[2,640,128]{2,1,0:T(8,128)S(1)} all-gather(f32[1,640,128]{2,1,0:T(8,128)S(1)} %bitcast.5), channel_id=1, replica_groups=mesh['x'=4,'y'=8,'z'=8,'c'=2] {'c'}, dimensions={0}, use_global_device_ids=true | all-gather | bytes 983040 | tf_op jit(solution)/shard_map/all_gather | solution.py:303
  68.7 13.9 %factor.1 = (f32[511,511]{1,0:T(8,128)}, f32[511]{0:T(512)}, f32[512,512]{1,0:T(8,128)}) custom-call(f32[2,640,128]{2,1,0:T(8,128)S(1)} %all_gather.3.g_ref, f32[512,512]{1,0:T(8,128)S(1)} %copy-done.1), custom_call_target="tpu_custom_call" | custom-call | tf_op jit(solution)/shard_map/factor/pallas_call | solution.py:262
  (4 shorter events, 0.1 us)
Async XLA Ops:
  0.6 1.2 %copy-start = (f32[512,512]{1,0:T(8,128)S(1)}, f32[512,512]{1,0:T(8,128)}, u32[]{:S(2)}) copy-start(f32[512,512]{1,0:T(8,128)} %x_ref.5) | copy-start | bytes 3145732
  1.9 9.7 %copy-start.1 = (f32[512,512]{1,0:T(8,128)S(1)}, f32[512,512]{1,0:T(8,128)}, u32[]{:S(2)}) copy-start(f32[512,512]{1,0:T(8,128)} %x_ref.5) | copy-start | bytes 3145732
  2.8 10.0 %collective-permute-start = (f32[640,128]{1,0:T(8,128)S(1)}, f32[640,128]{1,0:T(8,128)S(1)}, u32[]{:S(2)}, u32[]{:S(2)}) collective-permute-start(f32[640,128]{1,0:T(8,128)S(1)} %gram.3), channel_id=1, source_target_pairs={{0,1},{1,0},{2,3},{3,2},{4,5},{5,4},{6,7},{7,6},{8,9},{9,8},{10,11... | collective-permute-start | bytes 983048 | tf_op jit(solution)/shard_map/ppermute | solution.py:298

commit v5 on v4

--- a/solution.py
+++ b/solution.py
@@ -27,6 +27,33 @@
 def dot_high(x, y):
     return lax.dot_general(
         x, y, (((1,), (1,)), ((), ())), precision=lax.Precision.HIGH, preferred_element_type=F32
+    )
+
+
+def split3(x):
+    a = x.astype(BF)
+    rest = x - a.astype(F32)
+    b = rest.astype(BF)
+    c = (rest - b.astype(F32)).astype(BF)
+    return a, b, c
+
+
+def dot_joined(x, y, dims):
+    (i,), (j,) = dims
+    xa, xb, xc = split3(x)
+    ya, yb, yc = split3(y)
+    left = jnp.concatenate([xa, xa, xb, xb, xa, xc], i)
+    right = jnp.concatenate([ya, yb, ya, yb, yc, ya], j)
+    return lax.dot_general(left, right, (dims, ((), ())), preferred_element_type=F32)
+
+
+def dot_joined_high(x, y):
+    xa, xb, _ = split3(x)
+    ya, yb, _ = split3(y)
+    left = jnp.concatenate([xa, xa, xb], 1)
+    right = jnp.concatenate([ya, yb, ya], 1)
+    return lax.dot_general(
+        left, right, (((1,), (1,)), ((), ())), preferred_element_type=F32
     )
 
 
@@ -125,7 +152,9 @@
     return jnp.concatenate(ts, 0)
 
 
-def finish_kernel(scale, g_ref, x_ref, op_ref, co_ref, basis_ref, s_ref, h_ref, w_ref, y_ref, z_ref):
+def finish_kernel(
+    scale, g_ref, x_ref, op_ref, co_ref, basis_out, s_ref, h_ref, w_ref, y_ref, z_ref, basis_ref, sems
+):
     n, m = x_ref.shape
     nblk = m // NB
     span = [slice(i * NB, (i + 1) * NB) for i in range(nblk)]
@@ -144,7 +173,7 @@
 
     def op_block(i, j):
         k = slice(max(0, i - 1) * NB, (j + 1) * NB)
-        store_op(i, j, dot6(h_ref[span[i], k], w_ref[span[j], k], ((1,), (1,))))
+        store_op(i, j, dot_joined_high(h_ref[span[i], k], w_ref[span[j], k]))
 
     def tasks_after(b, t, r):
         o, e = b * NB, (b + 1) * NB
@@ -152,49 +181,55 @@
         tasks = []
 
         def panel(j):
-            r[j] = dot6(t, left_over(b, b, j), ((1,), (0,)))
+            r[j] = dot_joined(t, left_over(b, b, j), ((1,), (0,)))
 
         def trail(i, j):
-            s_ref[span[i], span[j]] = left_over(b, i, j) - dot6(r[i], r[j], ((0,), (0,)))
+            s_ref[span[i], span[j]] = left_over(b, i, j) - dot_joined(r[i], r[j], ((0,), (0,)))
 
         def own_inverse():
             if b > 0:
-                w_ref[o:e, :o] = dot6(t, w_ref[o:e, :o], ((1,), (0,)))
+                w_ref[o:e, :o] = dot_joined(t, w_ref[o:e, :o], ((1,), (0,)))
             w_ref[o:e, o:e] = t
 
         def later_inverse(i):
             if b > 0:
-                w_ref[span[i], :o] = w_ref[span[i], :o] - dot6(r[i], w_ref[o:e, :o], ((0,), (0,)))
-            w_ref[span[i], o:e] = -dot6(r[i], t, ((0,), (0,)))
+                w_ref[span[i], :o] = w_ref[span[i], :o] - dot_joined(r[i], w_ref[o:e, :o], ((0,), (0,)))
+            w_ref[span[i], o:e] = -dot_joined(r[i], t, ((0,), (0,)))
 
         def moved():
             row = lax.broadcasted_iota(jnp.int32, (NB, NB), 0)
             col = lax.broadcasted_iota(jnp.int32, (NB, NB), 1)
-            u = jnp.where(col >= row, dot6(t, left_over(b, b, b), ((1,), (0,))), 0.0)
+            u = jnp.where(col >= row, dot_joined(t, left_over(b, b, b), ((1,), (0,))), 0.0)
             pieces = ([jnp.zeros((NB, NB), F32)] if b else []) + [u] + [r[j] for j in later]
             row = jnp.concatenate(pieces, 1)
             h_ref[o:e, m - row.shape[1] :] = pltpu.roll(row, row.shape[1] - 1, 1)
 
         def basis(c):
             if b + 1 < nblk:
-                part = dot_high(x_ref[c : c + NB, :e], w_ref[o:e, :e])
+                part = dot_joined_high(x_ref[c : c + NB, :e], w_ref[o:e, :e])
             else:
-                part = dot_high(y_ref[c : c + NB, :], t)
+                part = dot_joined_high(y_ref[c : c + NB, :], t)
             basis_ref[c : c + NB, o:e] = part * scale
 
+        def send_basis():
+            copies.append(
+                pltpu.make_async_copy(basis_ref.at[:, span[b]], basis_out.at[:, span[b]], sems.at[b])
+            )
+            copies[-1].start()
+
         def basis_ahead(c):
-            y_ref[c : c + NB, :] = x_ref[c : c + NB, e:] + dot_high(
+            y_ref[c : c + NB, :] = x_ref[c : c + NB, e:] + dot_joined_high(
                 x_ref[c : c + NB, :e], w_ref[e:, :e]
             )
 
         def op_ahead(i):
             k = slice(max(0, i - 1) * NB, e)
-            z_ref[span[i], :] = h_ref[span[i], e:] + dot6(
-                h_ref[span[i], k], w_ref[e:, k], ((1,), (1,))
+            z_ref[span[i], :] = h_ref[span[i], e:] + dot_joined_high(
+                h_ref[span[i], k], w_ref[e:, k]
             )
 
         def op_last(i):
-            store_op(i, b, dot6(z_ref[span[i], :], t, ((1,), (1,))))
+            store_op(i, b, dot_joined_high(z_ref[span[i], :], t))
 
         for j in range(b + 2, nblk):
             tasks.append(functools.partial(panel, j))
@@ -207,6 +242,7 @@
         tasks.append(moved)
         for c in range(0, n, NB):
             tasks.append(functools.partial(basis, c))
+        tasks.append(send_basis)
         for i in range(b + 1):
             if b + 1 < nblk or i == b:
                 tasks.append(functools.partial(op_block, i, b))
@@ -223,6 +259,7 @@
             tasks.append(functools.partial(store_op, i, b, jnp.zeros((NB, NB), F32)))
         return tasks
 
+    copies = []
     tasks = []
     first = left_over(0, 0, 0)
     for b in range(nblk):
@@ -230,14 +267,16 @@
         t = factor_block(tiles, tasks)
         r = {}
         if b + 1 < nblk:
-            r[b + 1] = dot6(t, left_over(b, b, b + 1), ((1,), (0,)))
-            first = left_over(b, b + 1, b + 1) - dot6(r[b + 1], r[b + 1], ((0,), (0,)))
+            r[b + 1] = dot_joined(t, left_over(b, b, b + 1), ((1,), (0,)))
+            first = left_over(b, b + 1, b + 1) - dot_joined(r[b + 1], r[b + 1], ((0,), (0,)))
             s_ref[span[b + 1], span[b + 1]] = first
         tasks = tasks_after(b, t, r)
     for task in tasks:
         task()
     last = w_ref[m - 8 : m, :]
     co_ref[...] = (last * (-1.0 / last[7:8, m - 1 : m]))[7, : m - 1]
+    for copy in copies:
+        copy.wait()
 
 
 def local_gram(x, which, count):
@@ -267,7 +306,13 @@
             jax.ShapeDtypeStruct((n, m), F32),
         ),
         scratch_shapes=[pltpu.VMEM((m, m), F32)] * 3
-        + [pltpu.VMEM((n, NB), F32), pltpu.VMEM((m - NB, NB), F32)],
+        + [pltpu.VMEM((n, NB), F32), pltpu.VMEM((m - NB, NB), F32), pltpu.VMEM((n, m), F32)]
+        + [pltpu.SemaphoreType.DMA((m // NB,))],
+        out_specs=(
+            pl.BlockSpec(memory_space=pltpu.VMEM),
+            pl.BlockSpec(memory_space=pltpu.VMEM),
+            pl.BlockSpec(memory_space=pl.ANY),
+        ),
         compiler_params=pltpu.CompilerParams(vmem_limit_bytes=48 * 2**20),
         name="factor",
     )(gram, x)

time: 82.8 us -> 82.1 us (level)
  Pallas kernels: 15.7 us -> 14.8 us
    pallas_call x1, Pallas kernels: 13.9 us -> 13 us  [finish(): pl.pallas_call(functools.partial(finish_kernel, math.sqrt(rows_total)), o...]
where the time goes in v5:
time: 82.1 us; the launch traced here: 81.8 us
  blocking collectives  55.7 us (68%)
  Pallas kernels  14.8 us (18%)
  starting transfers between devices  8.8 us (11%)
  local copies, waits for them, and re-layouts  1.28 us (2%)
  between operations  0.85 us (1%)
    all_to_all x2, blocking collectives, swap(): lax.all_to_all(jnp.broadcast_to(part[None], (n,) + part.shape), axis, 0, 0)  34.6 us
    all_to_all x1, blocking collectives, scatter_sum(): return lax.all_to_all(part.reshape(n, -1, ROWS, NB), axis, 0, 0).sum(0)  14.6 us
    pallas_call x1, Pallas kernels, finish(): pl.pallas_call(functools.partial(finish_kernel, math.sqrt(rows_total)), o...  13 us
    ppermute x1, starting transfers between devices, body(): lax.ppermute(local_gram(snapshots, 1 - core, count), 'c', [(0, 1), (1, 0)])  8.8 us
    all_gather x1, blocking collectives, body(): gram = lax.all_gather(part, 'c')  6.48 us
    pallas_call x2, Pallas kernels, local_gram(): pl.pallas_call(gram_kernel, out_shape=jax.ShapeDtypeStruct((half_rows(m,...  1.8 us
  transfers between devices with their start and end apart: 1, of which 1 were waited for; matrix products, arithmetic and copies ran while one was open for 0% of the time, Pallas kernels for 1%

profile of v5, /device:TPU:1, one launch (start us, length us, event | category | flops | bytes accessed | tf_op | source)
XLA Modules:
  0.0 81.8 jit_solution(17161864876135336165)
XLA Ops:
  0.6 0.0 copy-start
  0.6 1.2 %copy-done = f32[512,512]{1,0:T(8,128)S(1)} copy-done((f32[512,512]{1,0:T(8,128)S(1)}, f32[512,512]{1,0:T(8,128)}, u32[]{:S(2)}) %copy-start) | copy-done | bytes 1048600
  1.9 0.0 copy-start.1
  1.9 0.9 %gram.3 = f32[640,128]{1,0:T(8,128)S(1)} custom-call(s32[1]{0:T(128)} %bitcast.1.which_ref, f32[512,512]{1,0:T(8,128)S(1)} %copy-done), custom_call_target="tpu_custom_call" | custom-call | flops 536870912 | bytes 1572864 | tf_op jit(solution)/shard_map/gram/pallas_call | solution.py:284
  2.8 8.8 %collective-permute-start = (f32[640,128]{1,0:T(8,128)S(1)}, f32[640,128]{1,0:T(8,128)S(1)}, u32[]{:S(2)}, u32[]{:S(2)}) collective-permute-start(f32[640,128]{1,0:T(8,128)S(1)} %gram.3), channel_id=1, source_target_pairs={{0,1},{1,0},{2,3},{3,2},{4,5},{5,4},{6,7},{7,6},{8,9},{9,8},{10,11... | collective-permute-start | bytes 983048 | tf_op jit(solution)/shard_map/ppermute | solution.py:343
  11.6 0.0 copy-done.1
  11.6 0.9 %gram.2 = f32[640,128]{1,0:T(8,128)S(1)} custom-call(s32[1]{0:T(128)} %bitcast.which_ref, f32[512,512]{1,0:T(8,128)S(1)} %copy-done.1), custom_call_target="tpu_custom_call" | custom-call | flops 536870912 | bytes 1572864 | tf_op jit(solution)/shard_map/gram/pallas_call | solution.py:284
  12.5 0.3 collective-permute-done
  12.8 14.6 %all_to_all.15 = f32[32,5,4,128]{3,2,1,0:T(4,128)S(1)} all-to-all(f32[32,5,4,128]{3,2,1,0:T(4,128)S(1)} %bitcast.4), channel_id=1, replica_groups=mesh['x'=4,'y'=8,'z'=8,'c'=2] {'x','y'}, dimensions={0} | all-to-all | bytes 655360 | tf_op jit(solution)/shard_map/all_to_all | solution.py:331
  27.4 0.1 reduce_sum.18
  27.5 17.2 %all_to_all.16 = f32[8,5,4,128]{3,2,1,0:T(4,128)S(1)} all-to-all(f32[8,5,4,128]{3,2,1,0:T(4,128)S(1)} %broadcast_in_dim.4), channel_id=1, replica_groups=mesh['x'=4,'y'=8,'z'=8,'c'=2] {'z'}, dimensions={0} | all-to-all | bytes 163840 | tf_op jit(solution)/shard_map/all_to_all | solution.py:336
  44.8 17.4 %all_to_all.17 = f32[32,5,4,128]{3,2,1,0:T(4,128)S(1)} all-to-all(f32[32,5,4,128]{3,2,1,0:T(4,128)S(1)} %broadcast_in_dim.5), channel_id=1, replica_groups=mesh['x'=4,'y'=8,'z'=8,'c'=2] {'x','y'}, dimensions={0} | all-to-all | bytes 655360 | tf_op jit(solution)/shard_map/all_to_all | solution.py:336
  62.2 6.5 %all_gather.3.g_ref = f32[2,640,128]{2,1,0:T(8,128)S(1)} all-gather(f32[1,640,128]{2,1,0:T(8,128)S(1)} %bitcast.5), channel_id=1, replica_groups=mesh['x'=4,'y'=8,'z'=8,'c'=2] {'c'}, dimensions={0}, use_global_device_ids=true | all-gather | bytes 983040 | tf_op jit(solution)/shard_map/all_gather | solution.py:348
  68.7 13.0 %factor.1 = (f32[511,511]{1,0:T(8,128)}, f32[511]{0:T(512)}, f32[512,512]{1,0:T(8,128)}) custom-call(f32[2,640,128]{2,1,0:T(8,128)S(1)} %all_gather.3.g_ref, f32[512,512]{1,0:T(8,128)S(1)} %copy-done.1), custom_call_target="tpu_custom_call" | custom-call | tf_op jit(solution)/shard_map/factor/pallas_call | solution.py:301
  (4 shorter events, 0.1 us)
Async XLA Ops:
  0.6 1.2 %copy-start = (f32[512,512]{1,0:T(8,128)S(1)}, f32[512,512]{1,0:T(8,128)}, u32[]{:S(2)}) copy-start(f32[512,512]{1,0:T(8,128)} %x_ref.5) | copy-start | bytes 3145732
  1.9 9.7 %copy-start.1 = (f32[512,512]{1,0:T(8,128)S(1)}, f32[512,512]{1,0:T(8,128)}, u32[]{:S(2)}) copy-start(f32[512,512]{1,0:T(8,128)} %x_ref.5) | copy-start | bytes 3145732
  2.8 10.0 %collective-permute-start = (f32[640,128]{1,0:T(8,128)S(1)}, f32[640,128]{1,0:T(8,128)S(1)}, u32[]{:S(2)}, u32[]{:S(2)}) collective-permute-start(f32[640,128]{1,0:T(8,128)S(1)} %gram.3), channel_id=1, source_target_pairs={{0,1},{1,0},{2,3},{3,2},{4,5},{5,4},{6,7},{7,6},{8,9},{9,8},{10,11... | collective-permute-start | bytes 983048 | tf_op jit(solution)/shard_map/ppermute | solution.py:343

commit v6 on v5

--- a/solution.py
+++ b/solution.py
@@ -76,7 +76,7 @@
             done = 0
             for i in sorted({i for i, _ in blocks}):
                 js = [j for k, j in blocks if k == i]
-                part = dot6(
+                part = dot_joined(
                     x_ref[:, i * NB : (i + 1) * NB],
                     x_ref[:, js[0] * NB : (js[-1] + 1) * NB],
                     ((0,), (0,)),

time: 82.1 us -> 82 us (level)
  no operation moved by 1% of the time
where the time goes in v6:
time: 82 us; the launch traced here: 81.7 us
  blocking collectives  55.7 us (68%)
  Pallas kernels  14.6 us (18%)
  starting transfers between devices  8.77 us (11%)
  local copies, waits for them, and re-layouts  1.28 us (2%)
  between operations  0.85 us (1%)
    all_to_all x2, blocking collectives, swap(): lax.all_to_all(jnp.broadcast_to(part[None], (n,) + part.shape), axis, 0, 0)  34.6 us
    all_to_all x1, blocking collectives, scatter_sum(): return lax.all_to_all(part.reshape(n, -1, ROWS, NB), axis, 0, 0).sum(0)  14.6 us
    pallas_call x1, Pallas kernels, finish(): pl.pallas_call(functools.partial(finish_kernel, math.sqrt(rows_total)), o...  13 us
    ppermute x1, starting transfers between devices, body(): lax.ppermute(local_gram(snapshots, 1 - core, count), 'c', [(0, 1), (1, 0)])  8.77 us
    all_gather x1, blocking collectives, body(): gram = lax.all_gather(part, 'c')  6.48 us
    pallas_call x2, Pallas kernels, local_gram(): pl.pallas_call(gram_kernel, out_shape=jax.ShapeDtypeStruct((half_rows(m,...  1.66 us
  transfers between devices with their start and end apart: 1, of which 1 were waited for; matrix products, arithmetic and copies ran while one was open for 0% of the time, Pallas kernels for 1%

profile of v6, /device:TPU:1, one launch (start us, length us, event | category | flops | bytes accessed | tf_op | source)
XLA Modules:
  0.0 81.7 jit_solution(13776444287240833884)
XLA Ops:
  0.6 0.0 copy-start
  0.6 1.2 %copy-done = f32[512,512]{1,0:T(8,128)S(1)} copy-done((f32[512,512]{1,0:T(8,128)S(1)}, f32[512,512]{1,0:T(8,128)}, u32[]{:S(2)}) %copy-start) | copy-done | bytes 1048600
  1.9 0.0 copy-start.1
  1.9 0.8 %gram.3 = f32[640,128]{1,0:T(8,128)S(1)} custom-call(s32[1]{0:T(128)} %bitcast.1.which_ref, f32[512,512]{1,0:T(8,128)S(1)} %copy-done), custom_call_target="tpu_custom_call" | custom-call | flops 536870912 | bytes 1572864 | tf_op jit(solution)/shard_map/gram/pallas_call | solution.py:284
  2.7 8.8 %collective-permute-start = (f32[640,128]{1,0:T(8,128)S(1)}, f32[640,128]{1,0:T(8,128)S(1)}, u32[]{:S(2)}, u32[]{:S(2)}) collective-permute-start(f32[640,128]{1,0:T(8,128)S(1)} %gram.3), channel_id=1, source_target_pairs={{0,1},{1,0},{2,3},{3,2},{4,5},{5,4},{6,7},{7,6},{8,9},{9,8},{10,11... | collective-permute-start | bytes 983048 | tf_op jit(solution)/shard_map/ppermute | solution.py:343
  11.5 0.0 copy-done.1
  11.5 0.8 %gram.2 = f32[640,128]{1,0:T(8,128)S(1)} custom-call(s32[1]{0:T(128)} %bitcast.which_ref, f32[512,512]{1,0:T(8,128)S(1)} %copy-done.1), custom_call_target="tpu_custom_call" | custom-call | flops 536870912 | bytes 1572864 | tf_op jit(solution)/shard_map/gram/pallas_call | solution.py:284
  12.3 0.4 collective-permute-done
  12.8 14.6 %all_to_all.15 = f32[32,5,4,128]{3,2,1,0:T(4,128)S(1)} all-to-all(f32[32,5,4,128]{3,2,1,0:T(4,128)S(1)} %bitcast.4), channel_id=1, replica_groups=mesh['x'=4,'y'=8,'z'=8,'c'=2] {'x','y'}, dimensions={0} | all-to-all | bytes 655360 | tf_op jit(solution)/shard_map/all_to_all | solution.py:331
  27.3 0.1 reduce_sum.18
  27.4 17.2 %all_to_all.16 = f32[8,5,4,128]{3,2,1,0:T(4,128)S(1)} all-to-all(f32[8,5,4,128]{3,2,1,0:T(4,128)S(1)} %broadcast_in_dim.4), channel_id=1, replica_groups=mesh['x'=4,'y'=8,'z'=8,'c'=2] {'z'}, dimensions={0} | all-to-all | bytes 163840 | tf_op jit(solution)/shard_map/all_to_all | solution.py:336
  44.7 17.4 %all_to_all.17 = f32[32,5,4,128]{3,2,1,0:T(4,128)S(1)} all-to-all(f32[32,5,4,128]{3,2,1,0:T(4,128)S(1)} %broadcast_in_dim.5), channel_id=1, replica_groups=mesh['x'=4,'y'=8,'z'=8,'c'=2] {'x','y'}, dimensions={0} | all-to-all | bytes 655360 | tf_op jit(solution)/shard_map/all_to_all | solution.py:336
  62.1 6.5 %all_gather.3.g_ref = f32[2,640,128]{2,1,0:T(8,128)S(1)} all-gather(f32[1,640,128]{2,1,0:T(8,128)S(1)} %bitcast.5), channel_id=1, replica_groups=mesh['x'=4,'y'=8,'z'=8,'c'=2] {'c'}, dimensions={0}, use_global_device_ids=true | all-gather | bytes 983040 | tf_op jit(solution)/shard_map/all_gather | solution.py:348
  68.6 13.0 %factor.1 = (f32[511,511]{1,0:T(8,128)}, f32[511]{0:T(512)}, f32[512,512]{1,0:T(8,128)}) custom-call(f32[2,640,128]{2,1,0:T(8,128)S(1)} %all_gather.3.g_ref, f32[512,512]{1,0:T(8,128)S(1)} %copy-done.1), custom_call_target="tpu_custom_call" | custom-call | tf_op jit(solution)/shard_map/factor/pallas_call | solution.py:301
  (4 shorter events, 0.1 us)
Async XLA Ops:
  0.6 1.2 %copy-start = (f32[512,512]{1,0:T(8,128)S(1)}, f32[512,512]{1,0:T(8,128)}, u32[]{:S(2)}) copy-start(f32[512,512]{1,0:T(8,128)} %x_ref.5) | copy-start | bytes 3145732
  1.9 9.6 %copy-start.1 = (f32[512,512]{1,0:T(8,128)S(1)}, f32[512,512]{1,0:T(8,128)}, u32[]{:S(2)}) copy-start(f32[512,512]{1,0:T(8,128)} %x_ref.5) | copy-start | bytes 3145732
  2.7 10.0 %collective-permute-start = (f32[640,128]{1,0:T(8,128)S(1)}, f32[640,128]{1,0:T(8,128)S(1)}, u32[]{:S(2)}, u32[]{:S(2)}) collective-permute-start(f32[640,128]{1,0:T(8,128)S(1)} %gram.3), channel_id=1, source_target_pairs={{0,1},{1,0},{2,3},{3,2},{4,5},{5,4},{6,7},{7,6},{8,9},{9,8},{10,11... | collective-permute-start | bytes 983048 | tf_op jit(solution)/shard_map/ppermute | solution.py:343
